TPU v7x, 32 devices: a whole 2x2x4 slice. The times are simulated.
32 devices in a mesh: cell: 2 (over x), dom: 16 (over z, y, core).
Axes of the slice: x: 2, y: 2, z: 4, core: 2. Of those that a mesh axis runs over, the one named last changes fastest.
Arguments:
- feats: bfloat16 [2, 2048, 128], P('cell', 'dom'), may hold values from -6 to 6
- positions: float32 [2, 3, 2048], P('cell', None, 'dom'), may hold values from 0 to 1
- species: int32 [2, 2048], P('cell', 'dom'), may hold values from 0 to 7
- wave_vectors: int32 [3, 2048], replicated, may hold values from -8 to 8, as said below
- smearing: float32 [128], replicated, may hold values from 0.001 to 0.03
- species_gain: float32 [8, 128], replicated, may hold values from 0.5 to 1.5
- w_charge: bfloat16 [128, 128], replicated, may hold values from -0.5 to 0.5
- w_message: bfloat16 [128, 128], replicated, may hold values from -0.5 to 0.5
- w_radial: float32 [8, 128], replicated, may hold values from -2 to 2
- w_out: bfloat16 [128, 128], replicated, may hold values from -0.5 to 0.5
- edge_sender: int32 [2, 196608], P('cell', 'dom'), may hold values from 0 to 191
- edge_receiver: int32 [2, 196608], P('cell', 'dom'), may hold values from 0 to 127
- edge_mask: int32 [2, 196608], P('cell', 'dom'), may hold values 0 or 1
- edge_length: float32 [2, 196608], P('cell', 'dom'), may hold values from 0.8 to 5.8
- ghost_down: int32 [2, 512], P('cell', 'dom'), may hold values from 0 to 127
- ghost_up: int32 [2, 512], P('cell', 'dom'), may hold values from 0 to 127
- cotangent: bfloat16 [2, 2048, 128], P('cell', 'dom'), may hold values from -6 to 6
Outputs:
- updated: bfloat16 [2, 2048, 128], P('cell', 'dom')
- feat_grad: bfloat16 [2, 2048, 128], P('cell', 'dom')
- grad_charge: float32 [128, 128], replicated
- grad_message: float32 [128, 128], replicated
- grad_radial: float32 [8, 128], replicated
- grad_out: float32 [128, 128], replicated
Inputs may be any that keep to these rules, and one draw needn't show every extreme that they name: `wave_vectors`: every column is a nonzero integer triple. `edge_sender`: rows below 128 are the domain's own atoms, then 32 rows from below, then 32 from above. `edge_receiver`: local row within the domain. `ghost_down`: local row within the sending domain; rows may repeat. `ghost_up`: local row within the sending domain; rows may repeat.
All inputs are finite; a program needn't handle non-finite values. No bound on the sum of `edge_mask` on one device may be relied on, other than what follows from the above.
Results may differ from a plain program's by a relative error of at most 0.01.
Values may be sent and summed in bfloat16 or wider, within the bound.
A program may use at most 64 MiB of HBM per device.

v0:
```python
import math

import jax
import jax.numpy as jnp
from jax import lax
from jax.sharding import PartitionSpec as P

cutoff_radius = 6.0
basis_width = 0.75
edge_scale = 0.25
filter_factor = 12.0


def extended_2(block, sides, width):
    for axis, dim in sides:
        count = lax.axis_size(axis)
        forward = [(i, i + 1) for i in range(count - 1)]
        forward.append((count - 1, 0))
        backward = [(target, source) for source, target in forward]
        low = lax.ppermute(
            lax.slice_in_dim(block, block.shape[dim] - width, None, axis=dim), axis, forward
        )
        high = lax.ppermute(lax.slice_in_dim(block, 0, width, axis=dim), axis, backward)
        block = jnp.concatenate([low, block, high], axis=dim)
    return block


def phase_tables(coords, wave_vectors):
    waves = wave_vectors.astype(jnp.float32)
    theta = (
        coords[0][:, None] * waves[0][None, :]
        + coords[1][:, None] * waves[1][None, :]
        + coords[2][:, None] * waves[2][None, :]
    )
    theta = 2.0 * math.pi * theta
    return (jnp.cos(theta).astype(jnp.bfloat16), jnp.sin(theta).astype(jnp.bfloat16))


def filter_table(wave_vectors, smearing):
    waves = wave_vectors.astype(jnp.float32)
    squared = jnp.sum(waves * waves, axis=0)
    return (
        filter_factor * jnp.exp(-squared[:, None] * smearing[None, :]) / jnp.sqrt(squared)[:, None]
    )


def radial_terms(lengths, w_radial):
    centers = 0.5 + basis_width * jnp.arange(w_radial.shape[0]).astype(jnp.float32)
    basis = jnp.exp(-jnp.square((lengths[:, None] - centers[None, :]) / basis_width))
    envelope = 0.5 * (jnp.cos(math.pi * lengths / cutoff_radius) + 1.0)
    radial = envelope[:, None] * jnp.dot(basis, w_radial, precision=lax.Precision.HIGHEST)
    return (basis, envelope, radial)


def contract_rows(left, right):
    return lax.dot_general(
        left, right, (((0,), (0,)), ((), ())), preferred_element_type=jnp.float32
    )


def reduced_field(local_re, local_im, filt, scale):
    total_re, total_im = lax.psum((local_re, local_im), "dom")
    return (
        (filt * total_re * scale).astype(jnp.bfloat16),
        (filt * total_im * scale).astype(jnp.bfloat16),
    )


def per_device(
    feats,
    positions,
    species,
    wave_vectors,
    smearing,
    species_gain,
    w_charge,
    w_message,
    w_radial,
    w_out,
    edge_sender,
    edge_receiver,
    edge_mask,
    edge_length,
    ghost_down,
    ghost_up,
    cotangent,
):
    own_rows = feats[0]
    coords = positions[0]
    senders = edge_sender[0]
    receivers = edge_receiver[0]
    live = edge_mask[0].astype(jnp.float32)[:, None]
    lengths = edge_length[0]
    downs = ghost_down[0]
    ups = ghost_up[0]
    upstream_cot = cotangent[0]
    atoms = own_rows.shape[0]
    ghosts = downs.shape[0]
    domains = lax.axis_size("dom")
    cells = lax.axis_size("cell")
    inv_waves = 1.0 / math.sqrt(wave_vectors.shape[1])
    inv_atoms = 1.0 / math.sqrt(atoms * domains)
    grad_scale = 1.0 / math.sqrt(cells * atoms * domains)
    labels = jnp.arange(species_gain.shape[0], dtype=jnp.int32)
    onehot = (species[0][:, None] == labels[None, :]).astype(jnp.float32)
    gain = jnp.dot(onehot, species_gain, precision=lax.Precision.HIGHEST)
    charges = (jnp.dot(own_rows, w_charge, preferred_element_type=jnp.float32) * gain).astype(
        jnp.bfloat16
    )
    outgoing = jnp.concatenate([own_rows[downs], own_rows[ups]], axis=0)
    padded = extended_2(outgoing, (("dom", 0),), ghosts)
    extended = jnp.concatenate([own_rows, padded[:ghosts], padded[3 * ghosts :]], axis=0)
    cos_table, sin_table = phase_tables(coords, wave_vectors)
    filt = filter_table(wave_vectors, smearing)
    field_re, field_im = reduced_field(
        contract_rows(cos_table, charges), contract_rows(sin_table, charges), filt, inv_atoms
    )
    potential = (
        jnp.dot(cos_table, field_re, preferred_element_type=jnp.float32)
        + jnp.dot(sin_table, field_im, preferred_element_type=jnp.float32)
    ) * inv_waves
    message_rows = jnp.dot(extended, w_message, preferred_element_type=jnp.float32).astype(
        jnp.bfloat16
    )
    basis, envelope, radial = radial_terms(lengths, w_radial)
    picked = message_rows[senders].astype(jnp.float32)
    messages = live * radial * picked
    aggregate = (
        jnp.zeros((atoms, message_rows.shape[1]), jnp.float32).at[receivers].add(messages)
        * edge_scale
    )
    preact = aggregate + potential
    act = jax.nn.silu(preact).astype(jnp.bfloat16)
    updated = (
        own_rows.astype(jnp.float32) + jnp.dot(act, w_out, preferred_element_type=jnp.float32)
    ).astype(jnp.bfloat16)
    grad_act = jnp.dot(upstream_cot, w_out.T, preferred_element_type=jnp.float32)
    sig = jax.nn.sigmoid(preact)
    grad_pre = grad_act * sig * (1.0 + preact * (1.0 - sig))
    grad_pre_b = grad_pre.astype(jnp.bfloat16)
    grad_out = contract_rows(act, upstream_cot)
    dfield_re, dfield_im = reduced_field(
        contract_rows(cos_table, grad_pre_b),
        contract_rows(sin_table, grad_pre_b),
        filt,
        inv_waves * inv_atoms,
    )
    grad_charges = jnp.dot(cos_table, dfield_re, preferred_element_type=jnp.float32) + jnp.dot(
        sin_table, dfield_im, preferred_element_type=jnp.float32
    )
    grad_raw = (grad_charges * gain).astype(jnp.bfloat16)
    grad_charge = contract_rows(own_rows, grad_raw)
    feat_from_charge = jnp.dot(grad_raw, w_charge.T, preferred_element_type=jnp.float32)
    upstream = grad_pre[receivers] * edge_scale
    grad_picked = live * radial * upstream
    grad_radial_edge = live * picked * upstream
    grad_msg = (
        jnp.zeros(message_rows.shape, jnp.float32).at[senders].add(grad_picked).astype(jnp.bfloat16)
    )
    grad_message = contract_rows(extended, grad_msg)
    grad_rows = jnp.dot(grad_msg, w_message.T, preferred_element_type=jnp.float32)
    grad_radial = jnp.dot(
        basis.T, envelope[:, None] * grad_radial_edge, precision=lax.Precision.HIGHEST
    )
    returning = grad_rows[atoms:]
    padded_back = extended_2(returning, (("dom", 0),), ghosts)
    own_total = upstream_cot.astype(jnp.float32) + feat_from_charge + grad_rows[:atoms]
    own_total = own_total.at[downs].add(padded_back[:ghosts]).at[ups].add(padded_back[3 * ghosts :])
    feat_grad = own_total.astype(jnp.bfloat16)
    partials = (grad_charge, grad_message, grad_radial, grad_out)
    totals = lax.psum((partials[0], partials[1], partials[2], partials[3]), ("cell", "dom"))
    return (
        updated[None],
        feat_grad[None],
        totals[0] * grad_scale,
        totals[1] * grad_scale,
        totals[2] * grad_scale,
        totals[3] * grad_scale,
    )


def solution(mesh):
    placed = (
        P("cell", "dom", None),
        P("cell", None, "dom"),
        P("cell", "dom"),
        P(),
        P(),
        P(),
        P(),
        P(),
        P(),
        P(),
        P("cell", "dom"),
        P("cell", "dom"),
        P("cell", "dom"),
        P("cell", "dom"),
        P("cell", "dom"),
        P("cell", "dom"),
        P("cell", "dom", None),
    )
    return jax.shard_map(
        per_device,
        mesh=mesh,
        in_specs=placed,
        out_specs=(P("cell", "dom", None), P("cell", "dom", None), P(), P(), P(), P()),
        check_vma=False,
    )
```

profile of v0, /device:TPU:0, one launch (start us, length us, event | category | flops | bytes accessed | tf_op | source)
XLA Modules:
  0.0 547.9 jit_solution(12469458019759251750)
XLA Ops:
  7.3 0.7 fusion.51
  8.0 0.6 copy-done.27
  8.5 1.3 gather_fusion.1
  9.9 5.5 %collective-permute-start.1 = (bf16[32,128]{1,0:T(8,128)(2,1)S(1)}, bf16[32,128]{1,0:T(8,128)(2,1)S(1)}, u32[]{:S(2)}, u32[]{:S(2)}) collective-permute-start(bf16[32,128]{1,0:T(8,128)(2,1)S(1)} %gather_fusion.1), channel_id=1, source_target_pairs={{1,0},{2,1},{3,2},{4,3},{5,4},{6,5},{7,6},{8,7},{9,8},{10,9},{11,1... | collective-permute-start | bytes 24584 | tf_op jit(solution)/shard_map/ppermute | solution.py:23
  15.4 0.7 fusion.50
  16.0 0.6 copy-done.29
  16.6 1.3 gather_fusion
  18.0 0.8 convert_element_type.79
  18.8 0.7 slice_bitcast_fusion.2
  19.5 0.9 fusion.35
  20.5 0.9 fusion.19
  21.4 4.8 fusion.67
  26.2 4.9 fusion.68
  31.2 0.2 all-reduce.9.cloned.1.call-start
  31.5 0.2 add_multiply_fusion.1
  31.8 0.6 copy-done.3
  32.4 0.6 broadcast_clamp_fusion.1
  33.1 19.4 %fusion = f32[12288,128]{1,0:T(8,128)} fusion(f32[8,128]{1,0:T(8,128)S(1)} %copy-done.25, f32[12288]{0:T(1024)S(1)} %add_multiply_fusion.1, f32[12288]{0:T(1024)S(1)} %bitcast.60, f32[8]{0:T(128)S(1)} %multiply_add_fusion, f32[12288]{0:T(1024)S(1)} %bitcast.63), kind=kOutput, calls=%fused_computation.9 | convolution fusion | flops 154533888 | bytes 6443040 | tf_op jit(solution)/shard_map/dot_general | solution.py:51
  52.7 0.4 copy-done.21
  53.2 41.8 %gather_fusion.2 = bf16[12288,128]{1,0:T(8,128)(2,1)S(1)} fusion(bf16[192,128]{1,0:T(8,128)(2,1)S(1)} %convolution_convert_fusion, s32[12288]{0:T(1024)} %broadcast_clamp_fusion.1), kind=kCustom, calls=%fused_computation.2 | custom fusion | bytes 6340608 | tf_op jit(solution)/shard_map/gather | solution.py:126
  95.0 66.5 %scatter_custom_fusion = f32[128,128]{1,0:T(8,128)S(1)} fusion(s32[12288]{0:T(1024)} %bitcast.68, f32[12288,128]{1,0:T(8,128)} %fusion, bf16[12288,128]{1,0:T(8,128)(2,1)S(1)} %gather_fusion.2, f32[]{:T(128)} %constant.15.clone.1), kind=kCustom, calls=%fused_computation.12 | custom fusion | flops 4718592 | bytes 9503232 | tf_op jit(solution)/shard_map/scatter-add | solution.py:129
  161.7 5.5 fusion.23
  167.2 4.2 fusion.18
  171.6 0.5 copy-done.46
  172.0 5.0 fusion.48
  177.1 4.8 fusion.46
  181.9 41.1 %gather_fusion.3 = f32[12288,128]{1,0:T(8,128)} fusion(f32[128,128]{1,0:T(8,128)S(1)} %fusion.16, s32[12288]{0:T(1024)S(1)} %broadcast_clamp_fusion), kind=kCustom, calls=%fused_computation.3 | custom fusion | bytes 12632064 | tf_op jit(solution)/shard_map/gather | solution.py:154
  223.0 12.7 %fusion.4 = f32[8,128]{1,0:T(8,128)S(1)} fusion(bf16[12288,128]{1,0:T(8,128)(2,1)S(1)} %gather_fusion.2, f32[12288,128]{1,0:T(8,128)} %gather_fusion.3, f32[12288]{0:T(1024)S(1)} %add_multiply_fusion.1, f32[12288]{0:T(1024)S(1)} %bitcast.61, f32[8]{0:T(128)} %copy-done.26, f32[12288]{0:T(1024)S(1)} %bitcast.64), kind=kOutput, calls=%fused_computation.15 | convolution fusion | flops 159252480 | bytes 9588768 | tf_op jit(solution)/shard_map/dot_general | solution.py:162
  235.9 66.8 %scatter_custom_fusion.1 = f32[192,128]{1,0:T(8,128)S(1)} fusion(s32[12288]{0:T(1024)} %bitcast.66, f32[12288,128]{1,0:T(8,128)} %fusion, f32[12288,128]{1,0:T(8,128)} %gather_fusion.3, f32[]{:T(128)} %constant.24.clone.1, f32[]{:T(128)} %constant.15.clone.1), kind=kCustom, calls=%fused_computation.16 | custom fusion | flops 4718592 | bytes 12682240 | tf_op jit(solution)/shard_map/scatter-add | solution.py:158
  303.0 4.5 collective-permute-start.3
  307.5 37.4 %psum.62 = f32[8,128]{1,0:T(8,128)S(1)} all-reduce(f32[8,128]{1,0:T(8,128)S(1)} %fusion.4), channel_id=1, replica_groups=mesh['cell'=2,'dom'=16] {'cell','dom'}, use_global_device_ids=true, to_apply=%region_11.12 | all-reduce | flops 1024 | bytes 8192 | tf_op jit(solution)/shard_map/psum | solution.py:171
  344.9 0.8 fusion.22
  345.7 0.6 broadcast_multiply_fusion.3
  346.3 0.8 fusion.37
  347.1 0.8 fusion.42
  348.0 54.4 %all-reduce.9.cloned.1.call-done = (f32[2048,128]{1,0:T(8,128)}, f32[2048,128]{1,0:T(8,128)}) async-done(((f32[2048,128]{1,0:T(8,128)}, f32[2048,128]{1,0:T(8,128)}), (f32[2048,128]{1,0:T(8,128)}, f32[2048,128]{1,0:T(8,128)})) %all-reduce.9.cloned.1.call-update) | async-done | bytes 2097168 | tf_op jit(solution)/shard_map/psum | solution.py:62
  402.5 5.4 fusion.24
  407.9 4.2 fusion.21
  412.2 0.8 convolution_bitcast_fusion
  413.1 0.8 scatter_fusion
  413.9 0.8 scatter_fusion.1
  414.7 0.6 convert_bitcast_fusion
  415.4 121.6 %all-reduce.7.cloned.1.call-done = (f32[128,128]{0,1:T(8,128)}, f32[128,128]{0,1:T(8,128)}, f32[128,128]{0,1:T(8,128)}) async-done(((f32[128,128]{0,1:T(8,128)}, f32[128,128]{0,1:T(8,128)}, f32[128,128]{0,1:T(8,128)}), (f32[128,128]{0,1:T(8,128)}, f32[128,128]{0,1:T(8,128)}, f32[128,128]{0,1:T(8,128)})) %all-reduce.7.cloned.1.call-update) | async-done | bytes 196624 | tf_op jit(solution)/shard_map/psum | solution.py:171
  537.0 0.8 broadcast_multiply_fusion.2
  537.8 0.7 copy.35
  538.5 0.9 broadcast_multiply_fusion
  539.4 0.7 copy.36
  540.2 0.7 copy.37
  (118 shorter events, 1.4 us)
Async XLA Ops:
  7.2 45.4 %copy-start = (bf16[128,128]{1,0:T(8,128)(2,1)S(1)}, bf16[128,128]{1,0:T(8,128)(2,1)}, u32[]{:S(2)}) copy-start(bf16[128,128]{1,0:T(8,128)(2,1)} %param.24) | copy-start | bytes 98308
  7.2 24.2 %copy-start.7 = (s32[1,12288]{1,0:T(1,128)S(1)}, s32[1,12288]{1,0:T(1,128)}, u32[]{:S(2)}) copy-start(s32[1,12288]{1,0:T(1,128)} %param.28) | copy-start | bytes 147460
  7.2 24.3 %copy-start.2 = (f32[1,12288]{1,0:T(1,128)S(1)}, f32[1,12288]{1,0:T(1,128)}, u32[]{:S(2)}) copy-start(f32[1,12288]{1,0:T(1,128)} %param.30) | copy-start | bytes 147460
  7.2 24.5 %copy-start.8 = (s32[1,12288]{1,0:T(1,128)S(1)}, s32[1,12288]{1,0:T(1,128)}, u32[]{:S(2)}) copy-start(s32[1,12288]{1,0:T(1,128)} %param.29) | copy-start | bytes 147460
  7.2 24.5 %copy-start.9 = (s32[1,12288]{1,0:T(1,128)S(1)}, s32[1,12288]{1,0:T(1,128)}, u32[]{:S(2)}) copy-start(s32[1,12288]{1,0:T(1,128)} %param.27) | copy-start | bytes 147460
  7.2 25.8 %copy-start.25 = (f32[8,128]{1,0:T(8,128)S(1)}, f32[8,128]{1,0:T(8,128)}, u32[]{:S(2)}) copy-start(f32[8,128]{1,0:T(8,128)} %param.25) | copy-start | bytes 12292
  7.2 154.3 %all-reduce.11.cloned.1.call-start = ((), (), s32[]{:S(2)}) async-start(), calls=%async_computation.2 | async-start | bytes 4194304 | tf_op jit(solution)/shard_map/psum | solution.py:62
  9.9 42.6 %collective-permute-start.1 = (bf16[32,128]{1,0:T(8,128)(2,1)S(1)}, bf16[32,128]{1,0:T(8,128)(2,1)S(1)}, u32[]{:S(2)}, u32[]{:S(2)}) collective-permute-start(bf16[32,128]{1,0:T(8,128)(2,1)S(1)} %gather_fusion.1), channel_id=1, source_target_pairs={{1,0},{2,1},{3,2},{4,3},{5,4},{6,5},{7,6},{8,7},{9,8},{10,9},{11,1... | collective-permute-start | bytes 24584 | tf_op jit(solution)/shard_map/ppermute | solution.py:23
  18.0 34.6 %collective-permute-start = (bf16[32,128]{1,0:T(8,128)(2,1)S(1)}, bf16[32,128]{1,0:T(8,128)(2,1)S(1)}, u32[]{:S(2)}, u32[]{:S(2)}) collective-permute-start(bf16[32,128]{1,0:T(8,128)(2,1)S(1)} %gather_fusion), channel_id=1, source_target_pairs={{0,1},{1,2},{2,3},{3,4},{4,5},{5,6},{6,7},{7,8},{8,9},{9,10},{10,1... | collective-permute-start | bytes 24584 | tf_op jit(solution)/shard_map/ppermute | solution.py:20
  18.8 12.3 %copy-start.18 = (f32[1,2048]{1,0:T(1,128)}, f32[1,2048]{1,0:T(1,128)S(1)}, u32[]{:S(2)}) copy-start(f32[1,2048]{1,0:T(1,128)S(1)} %get-tuple-element.35) | copy-start | bytes 24580
  18.8 12.7 %copy-start.12 = (f32[1,2048]{1,0:T(1,128)}, f32[1,2048]{1,0:T(1,128)S(1)}, u32[]{:S(2)}) copy-start(f32[1,2048]{1,0:T(1,128)S(1)} %get-tuple-element.33) | copy-start | bytes 24580
  18.8 12.7 %copy-start.15 = (f32[1,2048]{1,0:T(1,128)}, f32[1,2048]{1,0:T(1,128)S(1)}, u32[]{:S(2)}) copy-start(f32[1,2048]{1,0:T(1,128)S(1)} %get-tuple-element.34) | copy-start | bytes 24580
  19.5 11.6 %copy-start.31 = (f32[128]{0:T(128)}, f32[128]{0:T(128)S(1)}, u32[]{:S(2)}) copy-start(f32[128]{0:T(128)S(1)} %get-tuple-element.38) | copy-start | bytes 1540
  19.5 11.6 %copy-start.34 = (f32[128]{0:T(128)}, f32[128]{0:T(128)S(1)}, u32[]{:S(2)}) copy-start(f32[128]{0:T(128)S(1)} %get-tuple-element.39) | copy-start | bytes 1540
  19.5 11.6 %copy-start.37 = (f32[128]{0:T(128)}, f32[128]{0:T(128)S(1)}, u32[]{:S(2)}) copy-start(f32[128]{0:T(128)S(1)} %get-tuple-element.40) | copy-start | bytes 1540
  31.1 21.3 %copy-start.6 = (s32[3,2048]{1,0:T(4,128)S(1)}, s32[3,2048]{1,0:T(4,128)}, u32[]{:S(2)}) copy-start(s32[3,2048]{1,0:T(4,128)} %param.20) | copy-start | bytes 73732
  31.1 21.4 %copy-start.1 = (bf16[1,128,128]{2,1,0:T(8,128)(2,1)S(1)}, bf16[1,128,128]{2,1,0:T(8,128)(2,1)}, u32[]{:S(2)}) copy-start(bf16[1,128,128]{2,1,0:T(8,128)(2,1)} %param.17) | copy-start | bytes 98308
  31.2 371.2 %all-reduce.9.cloned.1.call-start = ((), (), s32[]{:S(2)}) async-start(), calls=%async_computation.1 | async-start | bytes 4194304 | tf_op jit(solution)/shard_map/psum | solution.py:62
  31.4 21.1 %copy-start.26 = (f32[8]{0:T(128)}, f32[8]{0:T(128)S(1)}, u32[]{:S(2)}) copy-start(f32[8]{0:T(128)S(1)} %multiply_add_fusion) | copy-start | bytes 100
  31.5 21.1 %copy-start.4 = (s32[12288,1]{0,1:T(1,128)}, s32[12288,1]{0,1:T(1,128)S(1)}, u32[]{:S(2)}) copy-start(s32[12288,1]{0,1:T(1,128)S(1)} %compare_select_fusion.1) | copy-start | bytes 147460
  161.6 5.6 %copy-start.13 = (f32[1,2048]{1,0:T(1,128)S(1)}, f32[1,2048]{1,0:T(1,128)}, u32[]{:S(2)}) copy-start(f32[1,2048]{1,0:T(1,128)} %copy-done.12) | copy-start | bytes 24580
  161.6 5.6 %copy-start.16 = (f32[1,2048]{1,0:T(1,128)S(1)}, f32[1,2048]{1,0:T(1,128)}, u32[]{:S(2)}) copy-start(f32[1,2048]{1,0:T(1,128)} %copy-done.15) | copy-start | bytes 24580
  161.6 5.6 %copy-start.19 = (f32[1,2048]{1,0:T(1,128)S(1)}, f32[1,2048]{1,0:T(1,128)}, u32[]{:S(2)}) copy-start(f32[1,2048]{1,0:T(1,128)} %copy-done.18) | copy-start | bytes 24580
  161.6 5.6 %copy-start.32 = (f32[128]{0:T(128)S(1)}, f32[128]{0:T(128)}, u32[]{:S(2)}) copy-start(f32[128]{0:T(128)} %copy-done.31) | copy-start | bytes 1540
  161.6 5.6 %copy-start.35 = (f32[128]{0:T(128)S(1)}, f32[128]{0:T(128)}, u32[]{:S(2)}) copy-start(f32[128]{0:T(128)} %copy-done.34) | copy-start | bytes 1540
  161.6 5.6 %copy-start.38 = (f32[128]{0:T(128)S(1)}, f32[128]{0:T(128)}, u32[]{:S(2)}) copy-start(f32[128]{0:T(128)} %copy-done.37) | copy-start | bytes 1540
  161.6 5.6 %copy-start.41 = (f32[2048,128]{1,0:T(8,128)S(1)}, f32[2048,128]{1,0:T(8,128)}, u32[]{:S(2)}) copy-start(f32[2048,128]{1,0:T(8,128)} %get-tuple-element.30) | copy-start | bytes 3145732
  161.6 5.6 %copy-start.44 = (f32[128]{0:T(128)S(1)}, f32[128]{0:T(128)}, u32[]{:S(2)}) copy-start(f32[128]{0:T(128)} %param.21) | copy-start | bytes 1540
  161.6 9.8 %copy-start.10 = (bf16[1,128,128]{2,1,0:T(8,128)(2,1)S(1)}, bf16[1,128,128]{2,1,0:T(8,128)(2,1)}, u32[]{:S(2)}) copy-start(bf16[1,128,128]{2,1,0:T(8,128)(2,1)} %param.33) | copy-start | bytes 98308
  161.6 9.8 %copy-start.42 = (bf16[128,128]{1,0:T(8,128)(2,1)S(1)}, bf16[128,128]{1,0:T(8,128)(2,1)}, u32[]{:S(2)}) copy-start(bf16[128,128]{1,0:T(8,128)(2,1)} %param.26) | copy-start | bytes 98308
  235.8 109.1 %copy-start.43 = (bf16[128,128]{1,0:T(8,128)(2,1)S(1)}, bf16[128,128]{1,0:T(8,128)(2,1)}, u32[]{:S(2)}) copy-start(bf16[128,128]{1,0:T(8,128)(2,1)} %param.26) | copy-start | bytes 98308
  235.8 109.1 %copy-start.47 = (f32[128,128]{1,0:T(8,128)S(1)}, f32[128,128]{1,0:T(8,128)}, u32[]{:S(2)}) copy-start(f32[128,128]{1,0:T(8,128)} %copy-done.46) | copy-start | bytes 196612
  235.8 110.5 %copy-start.11 = (bf16[1,128,128]{2,1,0:T(8,128)(2,1)S(1)}, bf16[1,128,128]{2,1,0:T(8,128)(2,1)}, u32[]{:S(2)}) copy-start(bf16[1,128,128]{2,1,0:T(8,128)(2,1)} %param.33) | copy-start | bytes 98308
  235.8 111.3 %copy-start.22 = (bf16[32,128]{1,0:T(8,128)(2,1)S(1)}, bf16[32,128]{1,0:T(8,128)(2,1)}, u32[]{:S(2)}) copy-start(bf16[32,128]{1,0:T(8,128)(2,1)} %copy-done.21) | copy-start | bytes 24580
  235.8 111.3 %copy-start.24 = (bf16[32,128]{1,0:T(8,128)(2,1)S(1)}, bf16[32,128]{1,0:T(8,128)(2,1)}, u32[]{:S(2)}) copy-start(bf16[32,128]{1,0:T(8,128)(2,1)} %copy-done.23) | copy-start | bytes 24580
  235.8 166.6 %copy-start.14 = (f32[1,2048]{1,0:T(1,128)S(1)}, f32[1,2048]{1,0:T(1,128)}, u32[]{:S(2)}) copy-start(f32[1,2048]{1,0:T(1,128)} %copy-done.12) | copy-start | bytes 24580
  235.8 166.6 %copy-start.17 = (f32[1,2048]{1,0:T(1,128)S(1)}, f32[1,2048]{1,0:T(1,128)}, u32[]{:S(2)}) copy-start(f32[1,2048]{1,0:T(1,128)} %copy-done.15) | copy-start | bytes 24580
  235.9 166.6 %copy-start.20 = (f32[1,2048]{1,0:T(1,128)S(1)}, f32[1,2048]{1,0:T(1,128)}, u32[]{:S(2)}) copy-start(f32[1,2048]{1,0:T(1,128)} %copy-done.18) | copy-start | bytes 24580
  235.9 166.6 %copy-start.33 = (f32[128]{0:T(128)S(1)}, f32[128]{0:T(128)}, u32[]{:S(2)}) copy-start(f32[128]{0:T(128)} %copy-done.31) | copy-start | bytes 1540
  235.9 166.6 %copy-start.36 = (f32[128]{0:T(128)S(1)}, f32[128]{0:T(128)}, u32[]{:S(2)}) copy-start(f32[128]{0:T(128)} %copy-done.34) | copy-start | bytes 1540
  235.9 166.6 %copy-start.39 = (f32[128]{0:T(128)S(1)}, f32[128]{0:T(128)}, u32[]{:S(2)}) copy-start(f32[128]{0:T(128)} %copy-done.37) | copy-start | bytes 1540
  235.9 166.6 %copy-start.45 = (f32[128]{0:T(128)S(1)}, f32[128]{0:T(128)}, u32[]{:S(2)}) copy-start(f32[128]{0:T(128)} %param.21) | copy-start | bytes 1540
  302.7 234.2 %all-reduce.7.cloned.1.call-start = ((), (), s32[]{:S(2)}) async-start(), calls=%async_computation | async-start | bytes 393216 | tf_op jit(solution)/shard_map/psum | solution.py:171
  302.9 110.2 %collective-permute-start.2 = (f32[32,128]{1,0:T(8,128)S(1)}, f32[32,128]{1,0:T(8,128)S(1)}, u32[]{:S(2)}, u32[]{:S(2)}) collective-permute-start(f32[32,128]{1,0:T(8,128)S(1)} %get-tuple-element.32), channel_id=1, source_target_pairs={{0,1},{1,2},{2,3},{3,4},{4,5},{5,6},{6,7},{7,8},{8,9},{9,10},{10,1... | collective-permute-start | bytes 49160 | tf_op jit(solution)/shard_map/ppermute | solution.py:20
  303.0 110.9 %collective-permute-start.3 = (f32[32,128]{1,0:T(8,128)S(1)}, f32[32,128]{1,0:T(8,128)S(1)}, u32[]{:S(2)}, u32[]{:S(2)}) collective-permute-start(f32[32,128]{1,0:T(8,128)S(1)} %get-tuple-element.31), channel_id=1, source_target_pairs={{1,0},{2,1},{3,2},{4,3},{5,4},{6,5},{7,6},{8,7},{9,8},{10,9},{11,1... | collective-permute-start | bytes 49160 | tf_op jit(solution)/shard_map/ppermute | solution.py:23
  402.5 9.6 %copy-start.5 = (bf16[128,128]{1,0:T(8,128)(2,1)S(1)}, bf16[128,128]{1,0:T(8,128)(2,1)}, u32[]{:S(2)}) copy-start(bf16[128,128]{1,0:T(8,128)(2,1)} %param.23) | copy-start | bytes 98308
  402.5 10.6 %copy-start.28 = (s32[32]{0:T(128)S(1)}, s32[32]{0:T(128)}, u32[]{:S(2)}) copy-start(s32[32]{0:T(128)} %copy-done.27) | copy-start | bytes 388
  402.5 11.5 %copy-start.30 = (s32[32]{0:T(128)S(1)}, s32[32]{0:T(128)}, u32[]{:S(2)}) copy-start(s32[32]{0:T(128)} %copy-done.29) | copy-start | bytes 388
  (7 other events, 9.1 us)
Sparse Core Ops, SparseCore 0:
  31.3 99.2 all-reduce.10
  302.8 99.5 all-reduce.8
  413.2 123.7 all-reduce.6
where the time goes:
time: 556 us; the launch traced here: 548 us
  waiting for transfers between devices  176 us (32%)
  other arithmetic  141 us (25%)
  local copies, waits for them, and re-layouts  91.4 us (16%)
  matrix products  76.6 us (14%)
  blocking collectives  37.4 us (7%)
  between operations  14.9 us (3%)
  starting transfers between devices  10.4 us (2%)
    psum x1, waiting for transfers between devices, per_device(): lax.psum((partials[0], partials[1], partials[2], partials[3]), ('cell', '...  122 us
    scatter-add x1, other arithmetic, per_device(): jnp.zeros(message_rows.shape, jnp.float32).at[senders].add(grad_picked)  66.8 us
    scatter-add x1, other arithmetic, per_device(): jnp.zeros((atoms, message_rows.shape[1]), jnp.float32).at[receivers]  66.5 us
    psum x2, waiting for transfers between devices, reduced_field(): total_re, total_im = lax.psum((local_re, local_im), 'dom')  54.4 us
    gather x1, local copies, waits for them, and re-layouts, per_device(): picked = message_rows[senders].astype(jnp.float32)  41.8 us
    gather x1, local copies, waits for them, and re-layouts, per_device(): upstream = grad_pre[receivers] * edge_scale  41.1 us
    psum x1, blocking collectives, per_device(): lax.psum((partials[0], partials[1], partials[2], partials[3]), ('cell', '...  37.4 us
    dot_general x7, matrix products, contract_rows(): lax.dot_general(left, right, (((0,), (0,)), ((), ())), preferred_element_...  22.1 us
  transfers between devices with their start and end apart: 7, of which 2 were waited for; matrix products, arithmetic and copies ran while one was open for 29% of the time, Pallas kernels for 0%

commit v1 on v0

--- a/solution.py
+++ b/solution.py
@@ -3,6 +3,8 @@
 import jax
 import jax.numpy as jnp
 from jax import lax
+from jax.experimental import pallas as pl
+from jax.experimental.pallas import tpu as pltpu
 from jax.sharding import PartitionSpec as P
 
 cutoff_radius = 6.0
@@ -44,14 +46,6 @@
     )
 
 
-def radial_terms(lengths, w_radial):
-    centers = 0.5 + basis_width * jnp.arange(w_radial.shape[0]).astype(jnp.float32)
-    basis = jnp.exp(-jnp.square((lengths[:, None] - centers[None, :]) / basis_width))
-    envelope = 0.5 * (jnp.cos(math.pi * lengths / cutoff_radius) + 1.0)
-    radial = envelope[:, None] * jnp.dot(basis, w_radial, precision=lax.Precision.HIGHEST)
-    return (basis, envelope, radial)
-
-
 def contract_rows(left, right):
     return lax.dot_general(
         left, right, (((0,), (0,)), ((), ())), preferred_element_type=jnp.float32
@@ -64,6 +58,56 @@
         (filt * total_re * scale).astype(jnp.bfloat16),
         (filt * total_im * scale).astype(jnp.bfloat16),
     )
+
+
+def pair_weights_kernel(senders, receivers, mask, lengths, out_ref, total, *, chunk, bases):
+    atoms = out_ref.shape[0] // bases
+    rows = out_ref.shape[1]
+    total[...] = jnp.zeros_like(total)
+
+    def body(step, carry):
+        at = pl.ds(pl.multiple_of(step * chunk, chunk), chunk)
+        length = lengths[:, at]
+        centers = 0.5 + basis_width * lax.broadcasted_iota(jnp.int32, (bases, chunk), 0).astype(
+            jnp.float32
+        )
+        basis = jnp.exp(-jnp.square((length - centers) / basis_width))
+        turn = math.pi * (length / cutoff_radius - 0.5)
+        square = turn * turn
+        sine = jnp.float32(-1.0 / 39916800.0)
+        for factor in (1.0 / 362880.0, -1.0 / 5040.0, 1.0 / 120.0, -1.0 / 6.0, 1.0):
+            sine = sine * square + factor
+        envelope = 0.5 * (1.0 - turn * sine) * mask[:, at].astype(jnp.float32)
+        weights = (basis * envelope).astype(jnp.bfloat16)
+        receiver = lax.broadcasted_iota(jnp.int32, (atoms, chunk), 0) == receivers[:, at]
+        sender = lax.broadcasted_iota(jnp.int32, (rows, chunk), 0) == senders[:, at]
+        receiver = receiver.astype(jnp.bfloat16)
+        sender = sender.astype(jnp.bfloat16)
+        left = jnp.concatenate([receiver * weights[b : b + 1] for b in range(bases)], axis=0)
+        total[...] += lax.dot_general(
+            left, sender, (((1,), (1,)), ((), ())), preferred_element_type=jnp.float32
+        )
+        return carry
+
+    lax.fori_loop(0, lengths.shape[1] // chunk, body, 0)
+    out_ref[...] = total[...].astype(out_ref.dtype)
+
+
+def pair_weights(senders, receivers, mask, lengths, atoms, rows, bases):
+    edges = lengths.shape[1]
+    shape = (bases * atoms, rows)
+    vmem = pl.BlockSpec(memory_space=pltpu.VMEM)
+    return pl.pallas_call(
+        lambda *refs: pair_weights_kernel(*refs, chunk=1024, bases=bases),
+        out_shape=jax.ShapeDtypeStruct(shape, jnp.bfloat16),
+        in_specs=[vmem] * 4,
+        out_specs=vmem,
+        scratch_shapes=[pltpu.VMEM(shape, jnp.float32)],
+        compiler_params=pltpu.CompilerParams(vmem_limit_bytes=48 * 1024 * 1024),
+        cost_estimate=pl.CostEstimate(
+            flops=2 * edges * shape[0] * rows, bytes_accessed=20 * edges, transcendentals=0
+        ),
+    )(senders, receivers, mask, lengths)
 
 
 def per_device(
@@ -87,10 +131,6 @@
 ):
     own_rows = feats[0]
     coords = positions[0]
-    senders = edge_sender[0]
-    receivers = edge_receiver[0]
-    live = edge_mask[0].astype(jnp.float32)[:, None]
-    lengths = edge_length[0]
     downs = ghost_down[0]
     ups = ghost_up[0]
     upstream_cot = cotangent[0]
@@ -122,13 +162,13 @@
     message_rows = jnp.dot(extended, w_message, preferred_element_type=jnp.float32).astype(
         jnp.bfloat16
     )
-    basis, envelope, radial = radial_terms(lengths, w_radial)
-    picked = message_rows[senders].astype(jnp.float32)
-    messages = live * radial * picked
-    aggregate = (
-        jnp.zeros((atoms, message_rows.shape[1]), jnp.float32).at[receivers].add(messages)
-        * edge_scale
-    )
+    bases = w_radial.shape[0]
+    pairs = pair_weights(
+        edge_sender, edge_receiver, edge_mask, edge_length, atoms, message_rows.shape[0], bases
+    )
+    mixed = jnp.dot(pairs, message_rows, preferred_element_type=jnp.float32)
+    mixed = mixed.reshape(bases, atoms, -1)
+    aggregate = jnp.sum(w_radial[:, None, :] * mixed, axis=0) * edge_scale
     preact = aggregate + potential
     act = jax.nn.silu(preact).astype(jnp.bfloat16)
     updated = (
@@ -151,17 +191,11 @@
     grad_raw = (grad_charges * gain).astype(jnp.bfloat16)
     grad_charge = contract_rows(own_rows, grad_raw)
     feat_from_charge = jnp.dot(grad_raw, w_charge.T, preferred_element_type=jnp.float32)
-    upstream = grad_pre[receivers] * edge_scale
-    grad_picked = live * radial * upstream
-    grad_radial_edge = live * picked * upstream
-    grad_msg = (
-        jnp.zeros(message_rows.shape, jnp.float32).at[senders].add(grad_picked).astype(jnp.bfloat16)
-    )
+    weighted = (w_radial[:, None, :] * (edge_scale * grad_pre)[None]).astype(jnp.bfloat16)
+    grad_msg = contract_rows(pairs, weighted.reshape(bases * atoms, -1)).astype(jnp.bfloat16)
     grad_message = contract_rows(extended, grad_msg)
     grad_rows = jnp.dot(grad_msg, w_message.T, preferred_element_type=jnp.float32)
-    grad_radial = jnp.dot(
-        basis.T, envelope[:, None] * grad_radial_edge, precision=lax.Precision.HIGHEST
-    )
+    grad_radial = jnp.sum(mixed * (edge_scale * grad_pre)[None], axis=1)
     returning = grad_rows[atoms:]
     padded_back = extended_2(returning, (("dom", 0),), ghosts)
     own_total = upstream_cot.astype(jnp.float32) + feat_from_charge + grad_rows[:atoms]

time: 556 us -> 403 us (0.72)
  other arithmetic: 141 us -> 4.49 us
  waiting for transfers between devices: 176 us -> 264 us
  local copies, waits for them, and re-layouts: 91.4 us -> 7.35 us
  matrix products: 76.6 us -> 54.4 us
  Pallas kernels: 0 us -> 9.15 us
    scatter-add x2 -> x0, other arithmetic: 133 us -> none  [the longest x1 66.8 us: per_device(): jnp.zeros(message_rows.shape, jnp.float32).at[senders].add(grad_picked)]
    psum x2, waiting for transfers between devices: 54.4 us -> 143 us  [reduced_field(): total_re, total_im = lax.psum((local_re, local_im), 'dom')]
    gather x2 -> x0, local copies, waits for them, and re-layouts: 82.9 us -> none  [the longest x1 41.8 us: per_device(): picked = message_rows[senders].astype(jnp.float32)]
    dot_general x3 -> x1, matrix products: 32.2 us -> 0.42 us  [per_device(): mixed = jnp.dot(pairs, message_rows, preferred_element_type=jnp.float32)]
    dot_general x7 -> x8, matrix products: 22.1 us -> 33.2 us  [contract_rows(): lax.dot_general(left, right, (((0,), (0,)), ((), ())), preferred_element_...]
    pallas_call x0 -> x1, Pallas kernels: none -> 9.15 us  [pair_weights(): pl.pallas_call(lambda *refs: pair_weights_kernel(*refs, chunk=1024, bases...]
  transfers between devices with their start and end apart: 7 -> 7, of which waited for: 2 -> 3; matrix products, arithmetic and copies ran while one was open for 29% -> 7% of each run, Pallas kernels for 0% -> 2%
where the time goes in v1:
time: 403 us; the launch traced here: 400 us
  waiting for transfers between devices  264 us (66%)
  matrix products  54.4 us (13%)
  blocking collectives  39.4 us (10%)
  between operations  14.2 us (4%)
  Pallas kernels  9.15 us (2%)
  local copies, waits for them, and re-layouts  7.35 us (2%)
  starting transfers between devices  6.66 us (2%)
  other arithmetic  4.49 us (1%)
    psum x2, waiting for transfers between devices, reduced_field(): total_re, total_im = lax.psum((local_re, local_im), 'dom')  143 us
    psum x1, waiting for transfers between devices, per_device(): lax.psum((partials[0], partials[1], partials[2], partials[3]), ('cell', '...  122 us
    psum x1, blocking collectives, per_device(): lax.psum((partials[0], partials[1], partials[2], partials[3]), ('cell', '...  39.4 us
    dot_general x8, matrix products, contract_rows(): lax.dot_general(left, right, (((0,), (0,)), ((), ())), preferred_element_...  33.2 us
    pallas_call x1, Pallas kernels, pair_weights(): pl.pallas_call(lambda *refs: pair_weights_kernel(*refs, chunk=1024, bases...  9.15 us
  transfers between devices with their start and end apart: 7, of which 3 were waited for; matrix products, arithmetic and copies ran while one was open for 7% of the time, Pallas kernels for 2%

profile of v1, /device:TPU:0, one launch (start us, length us, event | category | flops | bytes accessed | tf_op | source)
XLA Modules:
  0.0 400.1 jit_solution(7789037353118035583)
XLA Ops:
  7.2 0.7 fusion.27
  7.9 1.4 gather_fusion.1
  9.3 5.5 %collective-permute-start.1 = (bf16[32,128]{1,0:T(8,128)(2,1)S(1)}, bf16[32,128]{1,0:T(8,128)(2,1)S(1)}, u32[]{:S(2)}, u32[]{:S(2)}) collective-permute-start(bf16[32,128]{1,0:T(8,128)(2,1)S(1)} %gather_fusion.1), channel_id=1, source_target_pairs={{1,0},{2,1},{3,2},{4,3},{5,4},{6,5},{7,6},{8,7},{9,8},{10,9},{11,1... | collective-permute-start | bytes 24584 | tf_op jit(solution)/shard_map/ppermute | solution.py:25
  14.9 0.6 gather_fusion
  15.5 0.1 collective-permute-start
  15.5 0.1 copy-done.7
  15.7 0.6 copy-done.12
  16.3 0.2 fusion.16
  16.5 0.5 copy-done.6
  17.1 0.1 fusion.5
  17.2 4.9 %fusion.42 = f32[2048,128]{1,0:T(8,128)} fusion(bf16[128,128]{1,0:T(8,128)(2,1)S(1)} %fusion.5, f32[2048]{0:T(1024)S(1)} %bitcast.73, f32[128]{0:T(128)S(1)} %get-tuple-element.29, f32[2048]{0:T(1024)S(1)} %bitcast.81, f32[128]{0:T(128)S(1)} %get-tuple-element.30, f32[2048]{0:T(1024)S(1)} %bitcast.65, f32[128]{0:T(128)S(1)} %get-tuple-element.28), kind=kOutput, calls=%fused_computation.83 | convolution fusion | flops 68943872 | bytes 1107456 | tf_op jit(solution)/shard_map/dot_general | solution.py:50
  22.1 4.8 %fusion.41 = f32[2048,128]{1,0:T(8,128)} fusion(bf16[128,128]{1,0:T(8,128)(2,1)S(1)} %fusion.5, f32[2048]{0:T(1024)S(1)} %bitcast.74, f32[128]{0:T(128)S(1)} %get-tuple-element.29, f32[2048]{0:T(1024)S(1)} %bitcast.82, f32[128]{0:T(128)S(1)} %get-tuple-element.30, f32[2048]{0:T(1024)S(1)} %bitcast.66, f32[128]{0:T(128)S(1)} %get-tuple-element.28), kind=kOutput, calls=%fused_computation.82 | convolution fusion | flops 68943872 | bytes 1107456 | tf_op jit(solution)/shard_map/dot_general | solution.py:50
  26.9 0.0 all-reduce.9.cloned.1.call-start
  27.0 0.7 copy-done.1
  27.8 9.2 %shard_map.208 = bf16[1024,192]{1,0:T(8,128)(2,1)S(1)} custom-call(s32[1,12288]{1,0:T(1,128)S(1)} %copy-done.1, s32[1,12288]{1,0:T(1,128)S(1)} %copy-done.2, s32[1,12288]{1,0:T(1,128)S(1)} %copy-done.3, f32[1,12288]{1,0:T(1,128)S(1)} %copy-done.4), custom_call_target="tpu_custom_call" | custom-call | flops 4831838208 | bytes 245760 | tf_op jit(solution)/shard_map/pallas_call | solution.py:100
  37.0 0.4 fusion.8
  37.4 0.3 copy-done.11
  37.7 88.5 %all-reduce.11.cloned.1.call-done = (f32[2048,128]{1,0:T(8,128)}, f32[2048,128]{1,0:T(8,128)}) async-done(((f32[2048,128]{1,0:T(8,128)}, f32[2048,128]{1,0:T(8,128)}), (f32[2048,128]{1,0:T(8,128)}, f32[2048,128]{1,0:T(8,128)})) %all-reduce.11.cloned.1.call-update) | async-done | bytes 2097168 | tf_op jit(solution)/shard_map/psum | solution.py:56
  126.2 0.7 copy-done.19
  126.9 5.4 %fusion.10 = f32[128,128]{1,0:T(8,128)S(1)} fusion(f32[2048,128]{1,0:T(8,128)} %get-tuple-element.17, f32[2048]{0:T(1024)S(1)} %get-tuple-element.27, f32[128]{0:T(128)S(1)} %copy-done.19, f32[2048]{0:T(1024)S(1)} %get-tuple-element.26, f32[2048]{0:T(1024)S(1)} %bitcast.75, f32[128]{0:T(128)S(1)} %get-tuple-element.29, f32[2048]{0:T(1024)S(1)} %bitcast.83, ...), kind=kOutput, calls=%fused_computation.31 | convolution fusion | flops 70516736 | bytes 1157120 | tf_op jit(solution)/shard_map/dot_general | solution.py:159
  132.3 4.2 %fusion.4 = f32[128,128]{1,0:T(8,128)S(1)} fusion(f32[128,128]{1,0:T(8,128)S(1)} %fusion.10, f32[2048,128]{1,0:T(8,128)S(1)} %copy-done.16, f32[2048]{0:T(1024)S(1)} %get-tuple-element.27, f32[128]{0:T(128)S(1)} %copy-done.19, f32[2048]{0:T(1024)S(1)} %get-tuple-element.26, f32[128,128]{1,0:T(8,128)S(1)} %multiply_reduce_fusion.1, f32[2048]{0:T(1024)S(1)} %bitcast.76, ...), kind=kOutput, calls=%fused_computation.16 | convolution fusion | flops 70582272 | bytes 1288192 | tf_op jit(solution)/shard_map/dot_general | solution.py:160
  136.5 0.2 broadcast_multiply_fusion.3
  136.7 15.8 %fusion.22 = f32[2048,128]{1,0:T(8,128)} fusion(bf16[128,128]{1,0:T(8,128)(2,1)S(1)} %get-tuple-element.32, f32[2048]{0:T(1024)S(1)} %bitcast.77, f32[128]{0:T(128)S(1)} %get-tuple-element.29, f32[2048]{0:T(1024)S(1)} %bitcast.85, f32[128]{0:T(128)S(1)} %get-tuple-element.30, f32[2048]{0:T(1024)S(1)} %bitcast.69, f32[128]{0:T(128)S(1)} %get-tuple-element.28), kind=kOutput, calls=%fused_computation.56 | convolution fusion | flops 68943872 | bytes 1107456 | tf_op jit(solution)/shard_map/dot_general | solution.py:50
  152.5 4.8 %fusion.24 = f32[2048,128]{1,0:T(8,128)} fusion(bf16[128,128]{1,0:T(8,128)(2,1)S(1)} %get-tuple-element.32, f32[2048]{0:T(1024)S(1)} %bitcast.78, f32[128]{0:T(128)S(1)} %get-tuple-element.29, f32[2048]{0:T(1024)S(1)} %bitcast.86, f32[128]{0:T(128)S(1)} %get-tuple-element.30, f32[2048]{0:T(1024)S(1)} %bitcast.70, f32[128]{0:T(128)S(1)} %get-tuple-element.28), kind=kOutput, calls=%fused_computation.58 | convolution fusion | flops 68943872 | bytes 1107456 | tf_op jit(solution)/shard_map/dot_general | solution.py:50
  157.3 0.1 multiply_reduce_fusion
  157.4 0.3 convolution_convert_fusion
  157.8 0.0 all-reduce.7.cloned.1.call-start
  157.8 0.1 fusion.46
  158.0 1.0 collective-permute-start.3
  159.0 39.4 %psum.62 = f32[8,128]{1,0:T(8,128)S(1)} all-reduce(f32[8,128]{1,0:T(8,128)S(1)} %get-tuple-element.21), channel_id=1, replica_groups=mesh['cell'=2,'dom'=16] {'cell','dom'}, use_global_device_ids=true, to_apply=%region_11.12 | all-reduce | flops 1024 | bytes 8192 | tf_op jit(solution)/shard_map/psum | solution.py:205
  198.4 0.8 fusion.9
  199.2 0.6 broadcast_multiply_fusion.4
  199.8 0.8 fusion.21
  200.6 0.8 fusion.17
  201.5 54.3 %all-reduce.9.cloned.1.call-done = (f32[2048,128]{1,0:T(8,128)}, f32[2048,128]{1,0:T(8,128)}) async-done(((f32[2048,128]{1,0:T(8,128)}, f32[2048,128]{1,0:T(8,128)}), (f32[2048,128]{1,0:T(8,128)}, f32[2048,128]{1,0:T(8,128)})) %all-reduce.9.cloned.1.call-update) | async-done | bytes 2097168 | tf_op jit(solution)/shard_map/psum | solution.py:56
  255.7 5.4 %fusion.11 = f32[128,128]{1,0:T(8,128)S(1)} fusion(f32[2048,128]{1,0:T(8,128)} %get-tuple-element.15, f32[2048]{0:T(1024)S(1)} %get-tuple-element.27, f32[128]{0:T(128)S(1)} %copy-done.19, f32[2048]{0:T(1024)S(1)} %get-tuple-element.26, f32[2048]{0:T(1024)S(1)} %bitcast.79, f32[128]{0:T(128)S(1)} %get-tuple-element.29, f32[2048]{0:T(1024)S(1)} %bitcast.87, ...), kind=kOutput, calls=%fused_computation.32 | convolution fusion | flops 70516736 | bytes 1157120 | tf_op jit(solution)/shard_map/dot_general | solution.py:188
  261.2 4.2 %fusion.7 = bf16[128,128]{1,0:T(8,128)(2,1)S(1)} fusion(f32[128,128]{1,0:T(8,128)S(1)} %fusion.16, f32[128,128]{1,0:T(8,128)S(1)} %fusion.11, f32[2048,128]{1,0:T(8,128)S(1)} %copy-done.15, f32[2048]{0:T(1024)S(1)} %get-tuple-element.27, f32[128]{0:T(128)S(1)} %copy-done.19, f32[2048]{0:T(1024)S(1)} %get-tuple-element.26, f32[2048]{0:T(1024)S(1)} %bitcast.80, ...), kind=kOutput, calls=%fused_computation.20 | convolution fusion | flops 70565888 | bytes 1255424 | tf_op jit(solution)/shard_map/dot_general | solution.py:188
  265.3 0.1 fusion
  265.5 0.8 convolution_bitcast_fusion
  266.4 0.8 scatter_fusion
  267.2 0.8 scatter_fusion.1
  268.0 0.6 convert_bitcast_fusion
  268.6 121.6 %all-reduce.7.cloned.1.call-done = (f32[128,128]{0,1:T(8,128)}, f32[128,128]{0,1:T(8,128)}, f32[128,128]{0,1:T(8,128)}) async-done(((f32[128,128]{0,1:T(8,128)}, f32[128,128]{0,1:T(8,128)}, f32[128,128]{0,1:T(8,128)}), (f32[128,128]{0,1:T(8,128)}, f32[128,128]{0,1:T(8,128)}, f32[128,128]{0,1:T(8,128)})) %all-reduce.7.cloned.1.call-update) | async-done | bytes 196624 | tf_op jit(solution)/shard_map/psum | solution.py:205
  390.2 0.8 broadcast_multiply_fusion.2
  391.1 0.7 copy.25
  391.8 0.1 copy-done.8
  392.0 0.7 copy.27
  392.7 0.7 copy.26
  (53 shorter events, 0.4 us)
Async XLA Ops:
  7.2 29.8 %copy-start = (bf16[128,128]{1,0:T(8,128)(2,1)S(1)}, bf16[128,128]{1,0:T(8,128)(2,1)}, u32[]{:S(2)}) copy-start(bf16[128,128]{1,0:T(8,128)(2,1)} %param.24) | copy-start | bytes 98308
  7.2 119.0 %all-reduce.11.cloned.1.call-start = ((), (), s32[]{:S(2)}) async-start(), calls=%async_computation.2 | async-start | bytes 4194304 | tf_op jit(solution)/shard_map/psum | solution.py:56
  7.9 6.9 %copy-start.18 = (s32[1,32]{1,0:T(1,128)S(1)}, s32[1,32]{1,0:T(1,128)}, u32[]{:S(2)}) copy-start(s32[1,32]{1,0:T(1,128)} %param.32) | copy-start | bytes 388
  7.9 6.9 %copy-start.5 = (bf16[1,128,128]{2,1,0:T(8,128)(2,1)S(1)}, bf16[1,128,128]{2,1,0:T(8,128)(2,1)}, u32[]{:S(2)}) copy-start(bf16[1,128,128]{2,1,0:T(8,128)(2,1)} %param.17) | copy-start | bytes 98308
  9.3 27.6 %collective-permute-start.1 = (bf16[32,128]{1,0:T(8,128)(2,1)S(1)}, bf16[32,128]{1,0:T(8,128)(2,1)S(1)}, u32[]{:S(2)}, u32[]{:S(2)}) collective-permute-start(bf16[32,128]{1,0:T(8,128)(2,1)S(1)} %gather_fusion.1), channel_id=1, source_target_pairs={{1,0},{2,1},{3,2},{4,3},{5,4},{6,5},{7,6},{8,7},{9,8},{10,9},{11,1... | collective-permute-start | bytes 24584 | tf_op jit(solution)/shard_map/ppermute | solution.py:25
  14.8 0.7 copy-start.13
  14.8 0.8 copy-start.7
  15.5 21.5 %collective-permute-start = (bf16[32,128]{1,0:T(8,128)(2,1)S(1)}, bf16[32,128]{1,0:T(8,128)(2,1)S(1)}, u32[]{:S(2)}, u32[]{:S(2)}) collective-permute-start(bf16[32,128]{1,0:T(8,128)(2,1)S(1)} %gather_fusion), channel_id=1, source_target_pairs={{0,1},{1,2},{2,3},{3,4},{4,5},{5,6},{6,7},{7,8},{8,9},{9,10},{10,1... | collective-permute-start | bytes 24584 | tf_op jit(solution)/shard_map/ppermute | solution.py:22
  15.6 0.7 copy-start.12
  15.7 0.7 copy-start.14
  16.3 0.8 copy-start.6
  26.9 0.8 copy-start.1
  26.9 0.8 copy-start.2
  26.9 0.8 copy-start.3
  26.9 0.9 copy-start.4
  26.9 228.8 %all-reduce.9.cloned.1.call-start = ((), (), s32[]{:S(2)}) async-start(), calls=%async_computation.1 | async-start | bytes 4194304 | tf_op jit(solution)/shard_map/psum | solution.py:56
  37.0 0.7 copy-start.11
  126.2 0.7 copy-start.19
  126.9 5.4 %copy-start.16 = (f32[2048,128]{1,0:T(8,128)S(1)}, f32[2048,128]{1,0:T(8,128)}, u32[]{:S(2)}) copy-start(f32[2048,128]{1,0:T(8,128)} %get-tuple-element.18) | copy-start | bytes 3145732
  132.3 4.2 %copy-start.10 = (bf16[1,128,128]{2,1,0:T(8,128)(2,1)S(1)}, bf16[1,128,128]{2,1,0:T(8,128)(2,1)}, u32[]{:S(2)}) copy-start(bf16[1,128,128]{2,1,0:T(8,128)(2,1)} %param.33) | copy-start | bytes 98308
  132.3 4.2 %copy-start.17 = (bf16[128,128]{1,0:T(8,128)(2,1)S(1)}, bf16[128,128]{1,0:T(8,128)(2,1)}, u32[]{:S(2)}) copy-start(bf16[128,128]{1,0:T(8,128)(2,1)} %param.26) | copy-start | bytes 98308
  157.8 232.5 %all-reduce.7.cloned.1.call-start = ((), (), s32[]{:S(2)}) async-start(), calls=%async_computation | async-start | bytes 393216 | tf_op jit(solution)/shard_map/psum | solution.py:205
  158.0 109.2 %collective-permute-start.3 = (f32[32,128]{1,0:T(8,128)S(1)}, f32[32,128]{1,0:T(8,128)S(1)}, u32[]{:S(2)}, u32[]{:S(2)}) collective-permute-start(f32[32,128]{1,0:T(8,128)S(1)} %get-tuple-element.19), channel_id=1, source_target_pairs={{1,0},{2,1},{3,2},{4,3},{5,4},{6,5},{7,6},{8,7},{9,8},{10,9},{11,1... | collective-permute-start | bytes 49160 | tf_op jit(solution)/shard_map/ppermute | solution.py:25
  159.0 107.4 %collective-permute-start.2 = (f32[32,128]{1,0:T(8,128)S(1)}, f32[32,128]{1,0:T(8,128)S(1)}, u32[]{:S(2)}, u32[]{:S(2)}) collective-permute-start(f32[32,128]{1,0:T(8,128)S(1)} %get-tuple-element.20), channel_id=1, source_target_pairs={{0,1},{1,2},{2,3},{3,4},{4,5},{5,6},{6,7},{7,8},{8,9},{9,10},{10,1... | collective-permute-start | bytes 49160 | tf_op jit(solution)/shard_map/ppermute | solution.py:22
  255.7 5.4 %copy-start.15 = (f32[2048,128]{1,0:T(8,128)S(1)}, f32[2048,128]{1,0:T(8,128)}, u32[]{:S(2)}) copy-start(f32[2048,128]{1,0:T(8,128)} %get-tuple-element.16) | copy-start | bytes 3145732
  391.1 0.8 copy-start.8
  391.1 0.9 copy-start.9
Sparse Core Ops, SparseCore 0:
  27.1 99.1 all-reduce.10
  157.9 97.8 all-reduce.8
  266.5 123.7 all-reduce.6

commit v2 on v0

v2 whole, which is shorter than its diff:
```python
import functools
import math

import jax
import jax.numpy as jnp
from jax import lax
from jax.experimental import pallas as pl
from jax.experimental.pallas import tpu as pltpu
from jax.sharding import PartitionSpec as P

cutoff_radius = 6.0
basis_width = 0.75
edge_scale = 0.25
filter_factor = 12.0
MESH = pl.DeviceIdType.MESH
edge_chunk = 1024
wave_chunk = 128
lane = 128
part_rows = 8

sine_terms = (32.78140079, -74.47800454, 81.36681529, -41.33121431, 6.2830558)
cosine_terms = (-21.07678176, 58.79403849, -85.27239696, 64.92872661, -19.73898252, 0.99999922)


def horner(terms, x):
    value = terms[0] * x + terms[1]
    for term in terms[2:]:
        value = value * x + term
    return value


def dot(left, right, dims, precision=None):
    return lax.dot_general(
        left, right, (dims, ((), ())), preferred_element_type=jnp.float32, precision=precision
    )


def rows_by_rows(left, right):
    return dot(left, right, ((0,), (0,)))


def plain(left, right):
    return dot(left, right, ((1,), (0,)))


def by_transpose(left, right):
    return dot(left, right, ((1,), (1,)))


def edge_weights(length, mask, bases):
    shape = (bases, length.shape[1])
    centers = 0.5 + basis_width * lax.broadcasted_iota(jnp.int32, shape, 0).astype(jnp.float32)
    basis = jnp.exp(-jnp.square((length - centers) / basis_width))
    turn = math.pi * (length / cutoff_radius - 0.5)
    square = turn * turn
    sine = turn * horner(
        (-1.0 / 39916800.0, 1.0 / 362880.0, -1.0 / 5040.0, 1.0 / 120.0, -1.0 / 6.0, 1.0), square
    )
    return (basis * (0.5 * (1.0 - sine) * mask.astype(jnp.float32))).astype(jnp.bfloat16)


def spread(index, rows):
    shape = (rows, index.shape[1])
    return lax.broadcasted_iota(jnp.int32, shape, 0) == index


def block_kernel(
    domains,
    cells,
    feats,
    positions,
    species,
    waves,
    smearing,
    species_gain,
    w_charge,
    w_message,
    w_radial,
    w_out,
    senders,
    receivers,
    mask,
    lengths,
    ghost_down,
    ghost_up,
    cotangent,
    updated_ref,
    feat_grad_ref,
    grad_charge_ref,
    grad_message_ref,
    grad_radial_ref,
    grad_out_ref,
    pos_all,
    charge_all,
    grad_all,
    outgoing,
    extended,
    returning,
    returned,
    pair_total,
    pairs,
    points,
    wave_rows,
    table,
    own_table,
    field,
    half_out,
    half_in,
    sums_a,
    sums_b,
    slots_a,
    slots_b,
    reduced_a,
    reduced_b,
    owned_a,
    owned_b,
    gather_send,
    gather_recv,
    pass_send,
    pass_recv,
    side_send,
    side_recv,
    half_send,
    half_recv,
    weight_send,
    weight_recv,
):
    atoms = feats.shape[1]
    ghosts = ghost_down.shape[1]
    bases = w_radial.shape[0]
    wave_count = waves.shape[1]
    half = wave_count // 2
    chips = domains // 2
    devices = domains * cells
    inv_waves = 1.0 / math.sqrt(wave_count)
    inv_atoms = 1.0 / math.sqrt(atoms * domains)
    grad_scale = 1.0 / math.sqrt(cells * atoms * domains)

    cell = lax.axis_index("cell")
    me = lax.axis_index("dom")
    core = lax.rem(me, 2)
    chip = lax.div(me, 2)
    partner = me + 1 - 2 * core
    linear = cell * domains + me

    def place(index):
        return (lax.div(index, domains), lax.rem(index, domains))

    barrier = pltpu.get_barrier_semaphore()

    def greet(step, carry):
        target = lax.rem(linear + step, devices)
        pl.semaphore_signal(barrier, inc=1, device_id=place(target), device_id_type=MESH)
        return carry

    lax.fori_loop(1, devices, greet, 0)

    def remote(source, target, send, recv, index):
        return pltpu.make_async_remote_copy(
            src_ref=source,
            dst_ref=target,
            send_sem=send,
            recv_sem=recv,
            device_id=(cell, index),
            device_id_type=MESH,
        )

    rows = feats[0]
    upstream_cot = cotangent[0]
    pos_all[me] = jnp.zeros(pos_all.shape[1:], jnp.float32)
    pos_all[me, 0:3, :] = positions[0]
    kinds = spread(species[...], species_gain.shape[0]).astype(jnp.float32)
    gain = dot(kinds, species_gain[...], ((0,), (0,)), lax.Precision.HIGHEST)
    charge_all[me] = (plain(rows, w_charge[...]) * gain).astype(jnp.bfloat16)
    down_spread = spread(ghost_down[...], atoms).astype(jnp.bfloat16)
    up_spread = spread(ghost_up[...], atoms).astype(jnp.bfloat16)
    outgoing[0] = rows_by_rows(up_spread, rows).astype(jnp.bfloat16)
    outgoing[1] = rows_by_rows(down_spread, rows).astype(jnp.bfloat16)
    extended[0:atoms, :] = rows

    pl.semaphore_wait(barrier, devices - 1)

    def gather_copy(buffer, which, step, index):
        return remote(
            buffer.at[index],
            buffer.at[index],
            gather_send.at[which, step],
            gather_recv.at[which, step],
            lax.rem(chip + step, chips) * 2 + core,
        )

    def pass_copy(buffer, which, step, index):
        return remote(
            buffer.at[index],
            buffer.at[index],
            pass_send.at[which, step],
            pass_recv.at[which, step],
            partner,
        )

    def gather_start(buffer, which):
        pass_copy(buffer, which, 0, me).start()
        for step in range(1, chips):
            gather_copy(buffer, which, step, me).start()

    def gather_finish(buffer, which):
        for step in range(1, chips):
            source = lax.rem(chip - step + chips, chips) * 2 + core
            gather_copy(buffer, which, step, source).wait_recv()
            pass_copy(buffer, which, step, source).start()
        for step in range(chips):
            source = lax.rem(chip - step + chips, chips) * 2 + (1 - core)
            pass_copy(buffer, which, step, source).wait_recv()
        for step in range(1, chips):
            gather_copy(buffer, which, step, me).wait_send()
        for step in range(chips):
            pass_copy(buffer, which, step, me).wait_send()

    gather_start(pos_all, 0)
    gather_start(charge_all, 1)
    above = lax.rem(me + 1, domains)
    below = lax.rem(me + domains - 1, domains)
    low = pl.ds(atoms, ghosts)
    high = pl.ds(atoms + ghosts, ghosts)
    ghost_copies = [
        remote(outgoing.at[0], extended.at[low], side_send.at[0], side_recv.at[0], above),
        remote(outgoing.at[1], extended.at[high], side_send.at[1], side_recv.at[1], below),
    ]
    for copy in ghost_copies:
        copy.start()

    pair_total[...] = jnp.zeros_like(pair_total)

    def edge_step(step, carry):
        at = pl.ds(pl.multiple_of(step * edge_chunk, edge_chunk), edge_chunk)
        weights = edge_weights(lengths[:, at], mask[:, at], bases)
        receiver = spread(receivers[:, at], atoms).astype(jnp.bfloat16)
        sender = spread(senders[:, at], atoms + 2 * ghosts).astype(jnp.bfloat16)
        left = jnp.concatenate([receiver * weights[b : b + 1] for b in range(bases)], axis=0)
        pair_total[...] += by_transpose(left, sender)
        return carry

    lax.fori_loop(0, lengths.shape[1] // edge_chunk, edge_step, 0)
    pairs[...] = pair_total[...].astype(jnp.bfloat16)

    gather_finish(pos_all, 0)
    for index in range(domains):
        place_at = slice(index * atoms, (index + 1) * atoms)
        exact = pos_all[index]
        first = exact.astype(jnp.bfloat16)
        rest = exact - first.astype(jnp.float32)
        second = rest.astype(jnp.bfloat16)
        third = (rest - second.astype(jnp.float32)).astype(jnp.bfloat16)
        points[:, place_at] = jnp.concatenate(
            [first.astype(jnp.float32), second.astype(jnp.float32), third.astype(jnp.float32)],
            axis=0,
        ).astype(jnp.bfloat16)
    wave_rows[...] = jnp.zeros_like(wave_rows)
    wave_rows[0:3, :] = waves[
        :, pl.ds(pl.multiple_of(core * half, wave_chunk), half)
    ].astype(jnp.float32)
    pair_base = pl.multiple_of(chip * 2 * atoms, lane)
    gather_finish(charge_all, 1)
    charges = charge_all[...].reshape(domains * atoms, -1)
    ones = jnp.ones((part_rows, lane), jnp.bfloat16)

    def filter_of(at):
        wave = wave_rows[:, at]
        squared = rows_by_rows((wave * wave).astype(jnp.bfloat16), ones)
        return filter_factor * jnp.exp(-squared * smearing[...]) * lax.rsqrt(squared)

    def table_step(step, carry):
        at = pl.ds(pl.multiple_of(step * wave_chunk, wave_chunk), wave_chunk)
        then = pl.ds(pl.multiple_of(half + step * wave_chunk, wave_chunk), wave_chunk)
        wave = wave_rows[:, at]
        wave = jnp.concatenate([wave, wave, wave], axis=0).astype(jnp.bfloat16)
        turns = rows_by_rows(wave, points[...])
        turns = turns - jnp.floor(turns + 0.5)
        square = turns * turns
        cosine = horner(cosine_terms, square).astype(jnp.bfloat16)
        sine = (turns * horner(sine_terms, square)).astype(jnp.bfloat16)
        table[at, :] = cosine
        table[then, :] = sine
        scaled = filter_of(at) * inv_atoms
        field[at, :] = (scaled * plain(cosine, charges)).astype(jnp.bfloat16)
        field[then, :] = (scaled * plain(sine, charges)).astype(jnp.bfloat16)
        return carry

    lax.fori_loop(0, half // wave_chunk, table_step, 0)
    own_table[...] = table[:, pl.ds(pair_base, 2 * atoms)].T

    def exchange(which):
        partial = plain(own_table[...], field[...])
        half_out[which] = partial.reshape(2, atoms, -1)
        copy = remote(
            half_out.at[which, 1 - core],
            half_in.at[which],
            half_send.at[which],
            half_recv.at[which],
            partner,
        )
        copy.start()
        return copy

    first_exchange = exchange(0)
    for copy in ghost_copies:
        copy.wait()
    message_rows = plain(extended[...], w_message[...]).astype(jnp.bfloat16)
    mixed = plain(pairs[...], message_rows).reshape(bases, atoms, -1)
    aggregate = jnp.zeros((atoms, rows.shape[1]), jnp.float32)
    for b in range(bases):
        aggregate += w_radial[b : b + 1, :] * mixed[b]
    grad_act = by_transpose(upstream_cot, w_out[...])
    first_exchange.wait()
    potential = (half_out[0, core] + half_in[0]) * inv_waves
    preact = aggregate * edge_scale + potential
    sig = 1.0 / (1.0 + jnp.exp(-preact))
    grad_pre = grad_act * sig * (1.0 + preact * (1.0 - sig))
    grad_all[me] = grad_pre.astype(jnp.bfloat16)
    gather_start(grad_all, 2)

    act = (preact * sig).astype(jnp.bfloat16)
    updated_ref[0] = (rows.astype(jnp.float32) + plain(act, w_out[...])).astype(jnp.bfloat16)
    scaled_pre = edge_scale * grad_pre
    weighted = jnp.concatenate(
        [(w_radial[b : b + 1, :] * scaled_pre).astype(jnp.bfloat16) for b in range(bases)], axis=0
    )
    grad_msg = rows_by_rows(pairs[...], weighted).astype(jnp.bfloat16)
    grad_rows = by_transpose(grad_msg, w_message[...])
    returning[...] = grad_rows[atoms:].reshape(returning.shape)
    return_copies = [
        remote(returning.at[0], returned.at[0], side_send.at[2], side_recv.at[2], below),
        remote(returning.at[1], returned.at[1], side_send.at[3], side_recv.at[3], above),
    ]
    for copy in return_copies:
        copy.start()
    sums_a[0:atoms_of(sums_a), :] = rows_by_rows(extended[...], grad_msg)
    sums_a[atoms_of(sums_a) :, :] = rows_by_rows(act, upstream_cot)

    def scatter_start(sums, slots, which):
        owners = sums.shape[0] // part_rows
        slots[linear] = jnp.zeros(slots.shape[1:], jnp.float32)

        def send(step, carry):
            target = lax.rem(linear + step, devices)

            @pl.when(target < owners)
            def _():
                pltpu.make_async_remote_copy(
                    src_ref=sums.at[pl.ds(pl.multiple_of(target * part_rows, part_rows), part_rows)],
                    dst_ref=slots.at[linear],
                    send_sem=weight_send.at[which],
                    recv_sem=weight_recv.at[which],
                    device_id=place(target),
                    device_id_type=MESH,
                ).start()

            return carry

        lax.fori_loop(1, devices, send, 0)

    def wait_bytes(ref, send, recv):
        return pltpu.make_async_remote_copy(
            src_ref=ref,
            dst_ref=ref,
            send_sem=send,
            recv_sem=recv,
            device_id=(cell, partner),
            device_id_type=MESH,
        )

    def scatter_finish(sums, slots, owned, reduced, which):
        owners = sums.shape[0] // part_rows
        mine = pl.ds(pl.multiple_of(lax.rem(linear, owners) * part_rows, part_rows), part_rows)
        send, recv = weight_send.at[which], weight_recv.at[which]

        @pl.when(linear < owners)
        def _():
            wait_bytes(slots.at[pl.ds(0, devices - 1)], send, recv).wait_recv()
            wait_bytes(sums.at[pl.ds(0, (owners - 1) * part_rows)], send, recv).wait_send()
            total = sums[mine, :]
            for index in range(devices):
                total += slots[index]
            owned[...] = total * grad_scale
            reduced[mine, :] = owned[...]

        @pl.when(linear >= owners)
        def _():
            wait_bytes(sums, send, recv).wait_send()

    def share_start(owned, reduced, which):
        owners = reduced.shape[0] // part_rows

        @pl.when(linear < owners)
        def _():
            def send(step, carry):
                target = lax.rem(linear + step, devices)
                pltpu.make_async_remote_copy(
                    src_ref=owned,
                    dst_ref=reduced.at[
                        pl.ds(
                            pl.multiple_of(lax.rem(linear, owners) * part_rows, part_rows),
                            part_rows,
                        )
                    ],
                    send_sem=weight_send.at[which + 1],
                    recv_sem=weight_recv.at[which + 1],
                    device_id=place(target),
                    device_id_type=MESH,
                ).start()
                return carry

            lax.fori_loop(1, devices, send, 0)

    def share_finish(slots, reduced, which):
        owners = reduced.shape[0] // part_rows
        send, recv = weight_send.at[which + 1], weight_recv.at[which + 1]

        @pl.when(linear < owners)
        def _():
            wait_bytes(reduced.at[pl.ds(0, (owners - 1) * part_rows)], send, recv).wait_recv()
            wait_bytes(slots.at[pl.ds(0, devices - 1)], send, recv).wait_send()

        @pl.when(linear >= owners)
        def _():
            wait_bytes(reduced, send, recv).wait_recv()

    scatter_start(sums_a, slots_a, 0)

    grad_radial = jnp.concatenate(
        [jnp.sum(mixed[b] * scaled_pre, axis=0, keepdims=True) for b in range(bases)], axis=0
    )
    sums_b[pl.ds(sums_b.shape[0] - bases, bases), :] = grad_radial

    gather_finish(grad_all, 2)
    grads = grad_all[...].reshape(domains * atoms, -1)

    def back_step(step, carry):
        at = pl.ds(pl.multiple_of(step * wave_chunk, wave_chunk), wave_chunk)
        then = pl.ds(pl.multiple_of(half + step * wave_chunk, wave_chunk), wave_chunk)
        scaled = filter_of(at) * (inv_waves * inv_atoms)
        field[at, :] = (scaled * plain(table[at, :], grads)).astype(jnp.bfloat16)
        field[then, :] = (scaled * plain(table[then, :], grads)).astype(jnp.bfloat16)
        return carry

    lax.fori_loop(0, half // wave_chunk, back_step, 0)
    second_exchange = exchange(1)

    scatter_finish(sums_a, slots_a, owned_a, reduced_a, 0)
    share_start(owned_a, reduced_a, 0)

    second_exchange.wait()
    grad_raw = ((half_out[1, core] + half_in[1]) * gain).astype(jnp.bfloat16)
    sums_b[0 : sums_b.shape[0] - bases, :] = rows_by_rows(rows, grad_raw)
    scatter_start(sums_b, slots_b, 2)
    for copy in return_copies:
        copy.wait()
    total = (
        upstream_cot.astype(jnp.float32)
        + by_transpose(grad_raw, w_charge[...])
        + grad_rows[:atoms]
        + dot(down_spread.astype(jnp.float32), returned[1], ((1,), (0,)), lax.Precision.HIGHEST)
        + dot(up_spread.astype(jnp.float32), returned[0], ((1,), (0,)), lax.Precision.HIGHEST)
    )
    feat_grad_ref[0] = total.astype(jnp.bfloat16)

    scatter_finish(sums_b, slots_b, owned_b, reduced_b, 2)
    share_start(owned_b, reduced_b, 2)
    share_finish(slots_a, reduced_a, 0)
    grad_message_ref[...] = reduced_a[0 : atoms_of(sums_a), :]
    grad_out_ref[...] = reduced_a[atoms_of(sums_a) :, :]
    share_finish(slots_b, reduced_b, 2)
    grad_charge_ref[...] = reduced_b[0 : sums_b.shape[0] - bases, :]
    grad_radial_ref[...] = reduced_b[sums_b.shape[0] - bases :, :]


def atoms_of(sums):
    return sums.shape[0] // 2


def per_device(
    feats,
    positions,
    species,
    wave_vectors,
    smearing,
    species_gain,
    w_charge,
    w_message,
    w_radial,
    w_out,
    edge_sender,
    edge_receiver,
    edge_mask,
    edge_length,
    ghost_down,
    ghost_up,
    cotangent,
):
    domains = lax.axis_size("dom")
    cells = lax.axis_size("cell")
    atoms, width = feats.shape[1:]
    ghosts = ghost_down.shape[1]
    bases = w_radial.shape[0]
    wave_count = wave_vectors.shape[1]
    devices = domains * cells
    chips = domains // 2
    f32, bf16 = jnp.float32, jnp.bfloat16
    vmem = pl.BlockSpec(memory_space=pltpu.VMEM)
    count_a = 2 * width
    count_b = width + bases
    scratch = [
        pltpu.VMEM((domains, part_rows, atoms), f32),
        pltpu.VMEM((domains, atoms, width), bf16),
        pltpu.VMEM((domains, atoms, width), bf16),
        pltpu.VMEM((2, ghosts, width), bf16),
        pltpu.VMEM((atoms + 2 * ghosts, width), bf16),
        pltpu.VMEM((2, ghosts, width), f32),
        pltpu.VMEM((2, ghosts, width), f32),
        pltpu.VMEM((bases * atoms, atoms + 2 * ghosts), f32),
        pltpu.VMEM((bases * atoms, atoms + 2 * ghosts), bf16),
        pltpu.VMEM((3 * part_rows, domains * atoms), bf16),
        pltpu.VMEM((part_rows, wave_count // 2), f32),
        pltpu.VMEM((wave_count, domains * atoms), bf16),
        pltpu.VMEM((2 * atoms, wave_count), bf16),
        pltpu.VMEM((wave_count, width), bf16),
        pltpu.VMEM((2, 2, atoms, width), f32),
        pltpu.VMEM((2, atoms, width), f32),
        pltpu.VMEM((count_a, width), f32),
        pltpu.VMEM((count_b, width), f32),
        pltpu.VMEM((devices, part_rows, width), f32),
        pltpu.VMEM((devices, part_rows, width), f32),
        pltpu.VMEM((count_a, width), f32),
        pltpu.VMEM((count_b, width), f32),
        pltpu.VMEM((part_rows, width), f32),
        pltpu.VMEM((part_rows, width), f32),
        pltpu.SemaphoreType.DMA((3, chips)),
        pltpu.SemaphoreType.DMA((3, chips)),
        pltpu.SemaphoreType.DMA((3, chips)),
        pltpu.SemaphoreType.DMA((3, chips)),
        pltpu.SemaphoreType.DMA((4,)),
        pltpu.SemaphoreType.DMA((4,)),
        pltpu.SemaphoreType.DMA((2,)),
        pltpu.SemaphoreType.DMA((2,)),
        pltpu.SemaphoreType.DMA((4,)),
        pltpu.SemaphoreType.DMA((4,)),
    ]
    shape = jax.ShapeDtypeStruct
    return pl.pallas_call(
        functools.partial(block_kernel, domains, cells),
        out_shape=(
            shape(feats.shape, bf16),
            shape(feats.shape, bf16),
            shape((width, width), f32),
            shape((width, width), f32),
            shape((bases, width), f32),
            shape((width, width), f32),
        ),
        in_specs=[vmem] * 17,
        out_specs=(vmem,) * 6,
        scratch_shapes=scratch,
        compiler_params=pltpu.CompilerParams(
            collective_id=0, has_side_effects=True, vmem_limit_bytes=48 * 1024 * 1024
        ),
        name="ewald_block",
    )(
        feats,
        positions,
        species,
        wave_vectors,
        smearing[None, :],
        species_gain,
        w_charge,
        w_message,
        w_radial,
        w_out,
        edge_sender,
        edge_receiver,
        edge_mask,
        edge_length,
        ghost_down,
        ghost_up,
        cotangent,
    )


def solution(mesh):
    placed = (
        P("cell", "dom", None),
        P("cell", None, "dom"),
        P("cell", "dom"),
        P(),
        P(),
        P(),
        P(),
        P(),
        P(),
        P(),
        P("cell", "dom"),
        P("cell", "dom"),
        P("cell", "dom"),
        P("cell", "dom"),
        P("cell", "dom"),
        P("cell", "dom"),
        P("cell", "dom", None),
    )
    return jax.shard_map(
        per_device,
        mesh=mesh,
        in_specs=placed,
        out_specs=(P("cell", "dom", None), P("cell", "dom", None), P(), P(), P(), P()),
        check_vma=False,
    )
```

time: 556 us -> 72.6 us (0.13); the launches traced: 548 us -> 71.7 us
  waiting for transfers between devices: 176 us -> 0 us
  other arithmetic: 141 us -> 0 us
  local copies, waits for them, and re-layouts: 91.4 us -> 14.1 us
  matrix products: 76.6 us -> 0 us
  Pallas kernels: 0 us -> 56.9 us
  blocking collectives: 37.4 us -> 0 us
  between operations: 14.9 us -> 0.69 us
  starting transfers between devices: 10.4 us -> 0 us
    psum x3 -> x0, waiting for transfers between devices: 176 us -> none  [the longest x1 122 us: per_device(): lax.psum((partials[0], partials[1], partials[2], partials[3]), ('cell', '...]
    scatter-add x4 -> x0, other arithmetic: 135 us -> none  [the longest x1 66.8 us: per_device(): jnp.zeros(message_rows.shape, jnp.float32).at[senders].add(grad_picked)]
    gather x4 -> x0, local copies, waits for them, and re-layouts: 85.6 us -> none  [the longest x1 41.8 us: per_device(): picked = message_rows[senders].astype(jnp.float32)]
    dot_general x20 -> x0, matrix products: 76.6 us -> none  [the longest x7 22.1 us: contract_rows(): lax.dot_general(left, right, (((0,), (0,)), ((), ())), preferred_element_...]
    pallas_call x0 -> x1, Pallas kernels: none -> 56.9 us  [per_device(): pl.pallas_call(functools.partial(block_kernel, domains, cells), out_shape...]
    psum x1 -> x0, blocking collectives: 37.4 us -> none  [per_device(): lax.psum((partials[0], partials[1], partials[2], partials[3]), ('cell', '...]
    ppermute x4 -> x0, starting transfers between devices: 10.1 us -> none  [the longest x2 9.98 us: extended_2(): lax.ppermute(lax.slice_in_dim(block, 0, width, axis=dim), axis, backward)]
    unnamed x99 -> x39, local copies, waits for them, and re-layouts: 5.09 us -> 14.1 us
  transfers between devices with their start and end apart: 7 -> 0, of which waited for: 2 -> 0; matrix products, arithmetic and copies ran while one was open for 29% -> 0% of each run, Pallas kernels for 0% -> 0%
where the time goes in v2:
time: 72.6 us; the launch traced here: 71.7 us
  Pallas kernels  56.9 us (78%)
  local copies, waits for them, and re-layouts  14.1 us (19%)
    pallas_call x1, Pallas kernels, per_device(): pl.pallas_call(functools.partial(block_kernel, domains, cells), out_shape...  56.9 us
    unnamed x39, local copies, waits for them, and re-layouts  14.1 us

profile of v2, /device:TPU:0, one launch (start us, length us, event | category | flops | bytes accessed | tf_op | source)
XLA Modules:
  0.0 71.7 jit_solution(3279814238841674477)
XLA Ops:
  0.6 0.0 copy-start.10
  0.6 0.0 copy-start.12
  0.7 0.0 copy-start.13
  0.7 0.7 copy.23.positions
  1.4 0.0 copy-done.10
  1.4 0.0 copy-done.12
  1.4 0.0 copy-done.13
  1.4 0.0 copy-start
  1.4 0.8 %copy-done = s32[1,12288]{1,0:T(1,128)S(1)} copy-done((s32[1,12288]{1,0:T(1,128)S(1)}, s32[1,12288]{1,0:T(1,128)}, u32[]{:S(2)}) %copy-start) | copy-done | bytes 49176
  2.2 0.0 copy-start.1
  2.2 0.8 %copy-done.1 = s32[1,12288]{1,0:T(1,128)S(1)} copy-done((s32[1,12288]{1,0:T(1,128)S(1)}, s32[1,12288]{1,0:T(1,128)}, u32[]{:S(2)}) %copy-start.1) | copy-done | bytes 49176
  3.0 0.0 copy-start.2
  3.0 0.8 %copy-done.2 = s32[1,12288]{1,0:T(1,128)S(1)} copy-done((s32[1,12288]{1,0:T(1,128)S(1)}, s32[1,12288]{1,0:T(1,128)}, u32[]{:S(2)}) %copy-start.2) | copy-done | bytes 49176
  3.8 0.0 copy-start.3
  3.8 0.8 %copy-done.3 = f32[1,12288]{1,0:T(1,128)S(1)} copy-done((f32[1,12288]{1,0:T(1,128)S(1)}, f32[1,12288]{1,0:T(1,128)}, u32[]{:S(2)}) %copy-start.3) | copy-done | bytes 49176
  4.6 0.0 copy-start.4
  4.6 0.8 %copy-done.4 = bf16[1,128,128]{2,1,0:T(8,128)(2,1)S(1)} copy-done((bf16[1,128,128]{2,1,0:T(8,128)(2,1)S(1)}, bf16[1,128,128]{2,1,0:T(8,128)(2,1)}, u32[]{:S(2)}) %copy-start.4) | copy-done | bytes 32792
  5.3 0.0 copy-start.5
  5.3 0.8 %copy-done.5 = s32[3,2048]{1,0:T(4,128)S(1)} copy-done((s32[3,2048]{1,0:T(4,128)S(1)}, s32[3,2048]{1,0:T(4,128)}, u32[]{:S(2)}) %copy-start.5) | copy-done | bytes 24600
  6.1 0.0 copy-start.6
  6.1 0.8 %copy-done.6 = bf16[128,128]{1,0:T(8,128)(2,1)S(1)} copy-done((bf16[128,128]{1,0:T(8,128)(2,1)S(1)}, bf16[128,128]{1,0:T(8,128)(2,1)}, u32[]{:S(2)}) %copy-start.6) | copy-done | bytes 32792
  6.8 0.0 copy-start.7
  6.8 0.8 %copy-done.7 = bf16[128,128]{1,0:T(8,128)(2,1)S(1)} copy-done((bf16[128,128]{1,0:T(8,128)(2,1)S(1)}, bf16[128,128]{1,0:T(8,128)(2,1)}, u32[]{:S(2)}) %copy-start.7) | copy-done | bytes 32792
  7.6 0.0 copy-start.8
  7.6 0.8 %copy-done.8 = bf16[128,128]{1,0:T(8,128)(2,1)S(1)} copy-done((bf16[128,128]{1,0:T(8,128)(2,1)S(1)}, bf16[128,128]{1,0:T(8,128)(2,1)}, u32[]{:S(2)}) %copy-start.8) | copy-done | bytes 32792
  8.4 0.0 copy-start.9
  8.4 0.8 %copy-done.9 = bf16[1,128,128]{2,1,0:T(8,128)(2,1)S(1)} copy-done((bf16[1,128,128]{2,1,0:T(8,128)(2,1)S(1)}, bf16[1,128,128]{2,1,0:T(8,128)(2,1)}, u32[]{:S(2)}) %copy-start.9) | copy-done | bytes 32792
  9.1 0.0 copy-start.11
  9.1 0.7 copy-done.11
  9.8 0.0 copy-start.14
  9.8 0.7 copy-done.14
  10.5 0.0 copy-start.15
  10.5 0.7 copy-done.15
  11.1 56.9 %ewald_block.1 = (bf16[1,128,128]{2,1,0:T(8,128)(2,1)S(1)}, bf16[1,128,128]{2,1,0:T(8,128)(2,1)S(1)}, f32[128,128]{1,0:T(8,128)S(1)}, f32[128,128]{1,0:T(8,128)S...) custom-call(bf16[1,128,128]{2,1,0:T(8,128)(2,1)S(1)} %copy-done.4, f32[1,3,128]{2,1,0:T(4,128)S(1)} %copy.23.positions, ...), custom_call_target="tpu_custom_call" | custom-call | tf_op jit(solution)/shard_map/ewald_block/pallas_call | solution.py:549
  68.0 0.6 copy.30
  68.6 0.6 copy.31
  69.3 0.6 copy.32
  69.9 0.6 copy.33
  70.5 0.6 copy.34
  71.1 0.6 copy.35
Async XLA Ops:
  0.6 0.7 %copy-start.10 = (f32[8,128]{1,0:T(8,128)S(1)}, f32[8,128]{1,0:T(8,128)}, u32[]{:S(2)}) copy-start(f32[8,128]{1,0:T(8,128)} %species_gain.1) | copy-start | bytes 12292
  0.6 0.7 %copy-start.12 = (s32[1,128]{1,0:T(1,128)S(1)}, s32[1,128]{1,0:T(1,128)}, u32[]{:S(2)}) copy-start(s32[1,128]{1,0:T(1,128)} %species.1) | copy-start | bytes 1540
  0.7 0.7 copy-start.13
  1.4 0.8 %copy-start = (s32[1,12288]{1,0:T(1,128)S(1)}, s32[1,12288]{1,0:T(1,128)}, u32[]{:S(2)}) copy-start(s32[1,12288]{1,0:T(1,128)} %senders.1) | copy-start | bytes 147460
  2.2 0.8 %copy-start.1 = (s32[1,12288]{1,0:T(1,128)S(1)}, s32[1,12288]{1,0:T(1,128)}, u32[]{:S(2)}) copy-start(s32[1,12288]{1,0:T(1,128)} %receivers.1) | copy-start | bytes 147460
  3.0 0.8 %copy-start.2 = (s32[1,12288]{1,0:T(1,128)S(1)}, s32[1,12288]{1,0:T(1,128)}, u32[]{:S(2)}) copy-start(s32[1,12288]{1,0:T(1,128)} %mask.1) | copy-start | bytes 147460
  3.8 0.8 %copy-start.3 = (f32[1,12288]{1,0:T(1,128)S(1)}, f32[1,12288]{1,0:T(1,128)}, u32[]{:S(2)}) copy-start(f32[1,12288]{1,0:T(1,128)} %lengths.1) | copy-start | bytes 147460
  4.6 0.8 %copy-start.4 = (bf16[1,128,128]{2,1,0:T(8,128)(2,1)S(1)}, bf16[1,128,128]{2,1,0:T(8,128)(2,1)}, u32[]{:S(2)}) copy-start(bf16[1,128,128]{2,1,0:T(8,128)(2,1)} %feats.1) | copy-start | bytes 98308
  5.3 0.8 %copy-start.5 = (s32[3,2048]{1,0:T(4,128)S(1)}, s32[3,2048]{1,0:T(4,128)}, u32[]{:S(2)}) copy-start(s32[3,2048]{1,0:T(4,128)} %waves.1) | copy-start | bytes 73732
  6.1 0.8 %copy-start.6 = (bf16[128,128]{1,0:T(8,128)(2,1)S(1)}, bf16[128,128]{1,0:T(8,128)(2,1)}, u32[]{:S(2)}) copy-start(bf16[128,128]{1,0:T(8,128)(2,1)} %w_charge.1) | copy-start | bytes 98308
  6.8 0.8 %copy-start.7 = (bf16[128,128]{1,0:T(8,128)(2,1)S(1)}, bf16[128,128]{1,0:T(8,128)(2,1)}, u32[]{:S(2)}) copy-start(bf16[128,128]{1,0:T(8,128)(2,1)} %w_message.1) | copy-start | bytes 98308
  7.6 0.8 %copy-start.8 = (bf16[128,128]{1,0:T(8,128)(2,1)S(1)}, bf16[128,128]{1,0:T(8,128)(2,1)}, u32[]{:S(2)}) copy-start(bf16[128,128]{1,0:T(8,128)(2,1)} %w_out.1) | copy-start | bytes 98308
  8.4 0.8 %copy-start.9 = (bf16[1,128,128]{2,1,0:T(8,128)(2,1)S(1)}, bf16[1,128,128]{2,1,0:T(8,128)(2,1)}, u32[]{:S(2)}) copy-start(bf16[1,128,128]{2,1,0:T(8,128)(2,1)} %cotangent.1) | copy-start | bytes 98308
  9.1 0.7 copy-start.11
  9.8 0.7 copy-start.14
  10.5 0.7 copy-start.15

commit v3 on v2

--- a/solution.py
+++ b/solution.py
@@ -1,4 +1,3 @@
-import functools
 import math
 
 import jax
@@ -67,23 +66,8 @@
 def block_kernel(
     domains,
     cells,
-    feats,
-    positions,
-    species,
-    waves,
-    smearing,
-    species_gain,
-    w_charge,
-    w_message,
-    w_radial,
-    w_out,
-    senders,
-    receivers,
-    mask,
-    lengths,
-    ghost_down,
-    ghost_up,
-    cotangent,
+    sources,
+    staged,
     updated_ref,
     feat_grad_ref,
     grad_charge_ref,
@@ -99,8 +83,10 @@
     returned,
     pair_total,
     pairs,
-    points,
+    filt,
+    structure,
     wave_rows,
+    wave_columns,
     table,
     own_table,
     field,
@@ -124,7 +110,27 @@
     half_recv,
     weight_send,
     weight_recv,
+    load,
 ):
+    (
+        feats,
+        positions,
+        species,
+        waves,
+        smearing,
+        species_gain,
+        w_charge,
+        w_message,
+        w_radial,
+        w_out,
+        senders,
+        receivers,
+        mask,
+        lengths,
+        ghost_down,
+        ghost_up,
+        cotangent,
+    ) = staged
     atoms = feats.shape[1]
     ghosts = ghost_down.shape[1]
     bases = w_radial.shape[0]
@@ -146,6 +152,13 @@
     def place(index):
         return (lax.div(index, domains), lax.rem(index, domains))
 
+    loads = [
+        pltpu.make_async_copy(source, target, load.at[index])
+        for index, (source, target) in enumerate(zip(sources, staged))
+    ]
+    for copy in loads:
+        copy.start()
+
     barrier = pltpu.get_barrier_semaphore()
 
     def greet(step, carry):
@@ -153,7 +166,7 @@
         pl.semaphore_signal(barrier, inc=1, device_id=place(target), device_id_type=MESH)
         return carry
 
-    lax.fori_loop(1, devices, greet, 0)
+    lax.fori_loop(1, devices, greet, 0, unroll=devices <= 32)
 
     def remote(source, target, send, recv, index):
         return pltpu.make_async_remote_copy(
@@ -165,10 +178,12 @@
             device_id_type=MESH,
         )
 
+    for copy in loads:
+        copy.wait()
     rows = feats[0]
     upstream_cot = cotangent[0]
     pos_all[me] = jnp.zeros(pos_all.shape[1:], jnp.float32)
-    pos_all[me, 0:3, :] = positions[0]
+    pos_all[me, 0:3, :] = positions[:, 0, :]
     kinds = spread(species[...], species_gain.shape[0]).astype(jnp.float32)
     gain = dot(kinds, species_gain[...], ((0,), (0,)), lax.Precision.HIGHEST)
     charge_all[me] = (plain(rows, w_charge[...]) * gain).astype(jnp.bfloat16)
@@ -203,14 +218,18 @@
         for step in range(1, chips):
             gather_copy(buffer, which, step, me).start()
 
-    def gather_finish(buffer, which):
-        for step in range(1, chips):
-            source = lax.rem(chip - step + chips, chips) * 2 + core
-            gather_copy(buffer, which, step, source).wait_recv()
-            pass_copy(buffer, which, step, source).start()
-        for step in range(chips):
-            source = lax.rem(chip - step + chips, chips) * 2 + (1 - core)
-            pass_copy(buffer, which, step, source).wait_recv()
+    def chip_at(step):
+        return lax.rem(chip - step + chips, chips)
+
+    def gather_pass(buffer, which, step):
+        source = chip_at(step) * 2 + core
+        gather_copy(buffer, which, step, source).wait_recv()
+        pass_copy(buffer, which, step, source).start()
+
+    def gather_wait(buffer, which, step):
+        pass_copy(buffer, which, step, chip_at(step) * 2 + (1 - core)).wait_recv()
+
+    def gather_end(buffer, which):
         for step in range(1, chips):
             gather_copy(buffer, which, step, me).wait_send()
         for step in range(chips):
@@ -240,54 +259,65 @@
         pair_total[...] += by_transpose(left, sender)
         return carry
 
-    lax.fori_loop(0, lengths.shape[1] // edge_chunk, edge_step, 0)
+    edge_steps = lengths.shape[1] // edge_chunk
+    early_steps = edge_steps * 2 // 3
+    lax.fori_loop(0, early_steps, edge_step, 0)
+    for step in range(1, chips):
+        gather_pass(pos_all, 0, step)
+    for step in range(1, chips):
+        gather_pass(charge_all, 1, step)
+    lax.fori_loop(early_steps, edge_steps, edge_step, 0)
     pairs[...] = pair_total[...].astype(jnp.bfloat16)
 
-    gather_finish(pos_all, 0)
-    for index in range(domains):
-        place_at = slice(index * atoms, (index + 1) * atoms)
-        exact = pos_all[index]
-        first = exact.astype(jnp.bfloat16)
-        rest = exact - first.astype(jnp.float32)
-        second = rest.astype(jnp.bfloat16)
-        third = (rest - second.astype(jnp.float32)).astype(jnp.bfloat16)
-        points[:, place_at] = jnp.concatenate(
-            [first.astype(jnp.float32), second.astype(jnp.float32), third.astype(jnp.float32)],
-            axis=0,
-        ).astype(jnp.bfloat16)
     wave_rows[...] = jnp.zeros_like(wave_rows)
-    wave_rows[0:3, :] = waves[
-        :, pl.ds(pl.multiple_of(core * half, wave_chunk), half)
-    ].astype(jnp.float32)
-    pair_base = pl.multiple_of(chip * 2 * atoms, lane)
-    gather_finish(charge_all, 1)
-    charges = charge_all[...].reshape(domains * atoms, -1)
+    wave_rows[0:3, :] = waves[:, pl.ds(pl.multiple_of(core * half, lane), half)].astype(jnp.float32)
     ones = jnp.ones((part_rows, lane), jnp.bfloat16)
-
-    def filter_of(at):
-        wave = wave_rows[:, at]
-        squared = rows_by_rows((wave * wave).astype(jnp.bfloat16), ones)
-        return filter_factor * jnp.exp(-squared * smearing[...]) * lax.rsqrt(squared)
+    wave = wave_rows[...]
+    squared = rows_by_rows((wave * wave).astype(jnp.bfloat16), ones)
+    filt[...] = filter_factor * jnp.exp(-squared * smearing[...]) * lax.rsqrt(squared)
+    wave_columns[...] = jnp.concatenate([wave, wave, wave], axis=0).T.astype(jnp.bfloat16)
+    pair = 2 * atoms
+
+    def pair_of(step):
+        return pl.ds(chip_at(step) * 2, 2)
+
+    def columns(step):
+        return pl.ds(pl.multiple_of(step * pair, lane), pair)
 
     def table_step(step, carry):
-        at = pl.ds(pl.multiple_of(step * wave_chunk, wave_chunk), wave_chunk)
-        then = pl.ds(pl.multiple_of(half + step * wave_chunk, wave_chunk), wave_chunk)
-        wave = wave_rows[:, at]
-        wave = jnp.concatenate([wave, wave, wave], axis=0).astype(jnp.bfloat16)
-        turns = rows_by_rows(wave, points[...])
-        turns = turns - jnp.floor(turns + 0.5)
-        square = turns * turns
-        cosine = horner(cosine_terms, square).astype(jnp.bfloat16)
-        sine = (turns * horner(sine_terms, square)).astype(jnp.bfloat16)
-        table[at, :] = cosine
-        table[then, :] = sine
-        scaled = filter_of(at) * inv_atoms
-        field[at, :] = (scaled * plain(cosine, charges)).astype(jnp.bfloat16)
-        field[then, :] = (scaled * plain(sine, charges)).astype(jnp.bfloat16)
+        gather_wait(pos_all, 0, step)
+        block = pos_all[pair_of(step)]
+        exact = jnp.concatenate([block[0], block[1]], axis=1)
+        first = exact.astype(jnp.bfloat16).astype(jnp.float32)
+        rest = exact - first
+        second = rest.astype(jnp.bfloat16).astype(jnp.float32)
+        points = jnp.concatenate([first, second, rest - second], axis=0).astype(jnp.bfloat16)
+        at = columns(step)
+        for low_row in range(0, half, wave_chunk):
+            piece = slice(low_row, low_row + wave_chunk)
+            turns = plain(wave_columns[piece, :], points)
+            turns = turns - jnp.floor(turns + 0.5)
+            square = turns * turns
+            table[piece, at] = horner(cosine_terms, square).astype(jnp.bfloat16)
+            table[half + low_row : half + low_row + wave_chunk, at] = (
+                turns * horner(sine_terms, square)
+            ).astype(jnp.bfloat16)
+        gather_wait(charge_all, 1, step)
+        structure[...] += plain(table[:, at], charge_all[pair_of(step)].reshape(pair, -1))
         return carry
 
-    lax.fori_loop(0, half // wave_chunk, table_step, 0)
-    own_table[...] = table[:, pl.ds(pair_base, 2 * atoms)].T
+    structure[...] = jnp.zeros_like(structure)
+    lax.fori_loop(0, chips, table_step, 0)
+    own_table[...] = table[:, 0:pair].T
+
+    def fill_field(scale):
+        scaled = filt[...] * scale
+        field[0:half, :] = (scaled * structure[0:half, :]).astype(jnp.bfloat16)
+        field[half:, :] = (scaled * structure[half:, :]).astype(jnp.bfloat16)
+
+    fill_field(inv_atoms)
+    gather_end(pos_all, 0)
+    gather_end(charge_all, 1)
 
     def exchange(which):
         partial = plain(own_table[...], field[...])
@@ -357,7 +387,7 @@
 
             return carry
 
-        lax.fori_loop(1, devices, send, 0)
+        lax.fori_loop(1, devices, send, 0, unroll=devices <= 32)
 
     def wait_bytes(ref, send, recv):
         return pltpu.make_async_remote_copy(
@@ -410,7 +440,7 @@
                 ).start()
                 return carry
 
-            lax.fori_loop(1, devices, send, 0)
+            lax.fori_loop(1, devices, send, 0, unroll=devices <= 32)
 
     def share_finish(slots, reduced, which):
         owners = reduced.shape[0] // part_rows
@@ -432,18 +462,27 @@
     )
     sums_b[pl.ds(sums_b.shape[0] - bases, bases), :] = grad_radial
 
-    gather_finish(grad_all, 2)
-    grads = grad_all[...].reshape(domains * atoms, -1)
+    ahead = min(2, chips - 1)
+    for step in range(1, ahead + 1):
+        gather_pass(grad_all, 2, step)
+    structure[...] = jnp.zeros_like(structure)
 
     def back_step(step, carry):
-        at = pl.ds(pl.multiple_of(step * wave_chunk, wave_chunk), wave_chunk)
-        then = pl.ds(pl.multiple_of(half + step * wave_chunk, wave_chunk), wave_chunk)
-        scaled = filter_of(at) * (inv_waves * inv_atoms)
-        field[at, :] = (scaled * plain(table[at, :], grads)).astype(jnp.bfloat16)
-        field[then, :] = (scaled * plain(table[then, :], grads)).astype(jnp.bfloat16)
+        @pl.when(step + ahead < chips)
+        def _():
+            @pl.when(step > 0)
+            def _():
+                gather_pass(grad_all, 2, step + ahead)
+
+        gather_wait(grad_all, 2, step)
+        structure[...] += plain(
+            table[:, columns(step)], grad_all[pair_of(step)].reshape(pair, -1)
+        )
         return carry
 
-    lax.fori_loop(0, half // wave_chunk, back_step, 0)
+    lax.fori_loop(0, chips, back_step, 0)
+    fill_field(inv_waves * inv_atoms)
+    gather_end(grad_all, 2)
     second_exchange = exchange(1)
 
     scatter_finish(sums_a, slots_a, owned_a, reduced_a, 0)
@@ -476,6 +515,19 @@
 
 def atoms_of(sums):
     return sums.shape[0] // 2
+
+
+def write_kernel(*refs):
+    done = refs[-1]
+    count = len(refs) // 2
+    copies = [
+        pltpu.make_async_copy(refs[index], refs[count + index], done.at[index])
+        for index in range(count)
+    ]
+    for copy in copies:
+        copy.start()
+    for copy in copies:
+        copy.wait()
 
 
 def per_device(
@@ -519,8 +571,10 @@
         pltpu.VMEM((2, ghosts, width), f32),
         pltpu.VMEM((bases * atoms, atoms + 2 * ghosts), f32),
         pltpu.VMEM((bases * atoms, atoms + 2 * ghosts), bf16),
-        pltpu.VMEM((3 * part_rows, domains * atoms), bf16),
+        pltpu.VMEM((wave_count // 2, width), f32),
+        pltpu.VMEM((wave_count, width), f32),
         pltpu.VMEM((part_rows, wave_count // 2), f32),
+        pltpu.VMEM((wave_count // 2, 3 * part_rows), bf16),
         pltpu.VMEM((wave_count, domains * atoms), bf16),
         pltpu.VMEM((2 * atoms, wave_count), bf16),
         pltpu.VMEM((wave_count, width), bf16),
@@ -546,26 +600,9 @@
         pltpu.SemaphoreType.DMA((4,)),
     ]
     shape = jax.ShapeDtypeStruct
-    return pl.pallas_call(
-        functools.partial(block_kernel, domains, cells),
-        out_shape=(
-            shape(feats.shape, bf16),
-            shape(feats.shape, bf16),
-            shape((width, width), f32),
-            shape((width, width), f32),
-            shape((bases, width), f32),
-            shape((width, width), f32),
-        ),
-        in_specs=[vmem] * 17,
-        out_specs=(vmem,) * 6,
-        scratch_shapes=scratch,
-        compiler_params=pltpu.CompilerParams(
-            collective_id=0, has_side_effects=True, vmem_limit_bytes=48 * 1024 * 1024
-        ),
-        name="ewald_block",
-    )(
+    operands = (
         feats,
-        positions,
+        positions.transpose(1, 0, 2),
         species,
         wave_vectors,
         smearing[None, :],
@@ -582,6 +619,43 @@
         ghost_up,
         cotangent,
     )
+    count = len(operands)
+    staged = [pltpu.VMEM(value.shape, value.dtype) for value in operands]
+    scratch = [*staged, *scratch, pltpu.SemaphoreType.DMA((count,))]
+    outs = (
+        shape(feats.shape, bf16),
+        shape(feats.shape, bf16),
+        shape((width, width), f32),
+        shape((width, width), f32),
+        shape((bases, width), f32),
+        shape((width, width), f32),
+    )
+
+    def body(*refs):
+        sources, rest = refs[:count], refs[count:]
+        results, rest = rest[: len(outs)], rest[len(outs) :]
+        block_kernel(domains, cells, sources, rest[:count], *results, *rest[count:])
+
+    results = pl.pallas_call(
+        body,
+        out_shape=outs,
+        in_specs=[pl.BlockSpec(memory_space=pltpu.HBM)] * count,
+        out_specs=(vmem,) * len(outs),
+        scratch_shapes=scratch,
+        compiler_params=pltpu.CompilerParams(
+            collective_id=0, has_side_effects=True, vmem_limit_bytes=64 * 1024 * 1024
+        ),
+        name="ewald_block",
+    )(*operands)
+    return pl.pallas_call(
+        write_kernel,
+        out_shape=outs,
+        in_specs=[pl.BlockSpec(memory_space=pltpu.HBM)] * len(outs),
+        out_specs=(pl.BlockSpec(memory_space=pltpu.HBM),) * len(outs),
+        scratch_shapes=[pltpu.SemaphoreType.DMA((len(outs),))],
+        compiler_params=pltpu.CompilerParams(vmem_limit_bytes=64 * 1024 * 1024),
+        name="write_out",
+    )(*results)
 
 
 def solution(mesh):

time: 72.6 us -> 67.3 us (0.927)
  local copies, waits for them, and re-layouts: 14.1 us -> 0 us
  Pallas kernels: 56.9 us -> 66.5 us
    unnamed x39 -> x0, local copies, waits for them, and re-layouts: 14.1 us -> none
    pallas_call x1 -> x2, Pallas kernels: 56.9 us -> 66.5 us  [the longest x1 57.3 us: per_device(): pl.pallas_call(body, out_shape=outs, in_specs=[pl.BlockSpec(memory_space=...]
where the time goes in v3:
time: 67.3 us; the launch traced here: 67.1 us
  Pallas kernels  66.5 us (99%)
    pallas_call x1, Pallas kernels, per_device(): pl.pallas_call(body, out_shape=outs, in_specs=[pl.BlockSpec(memory_space=...  57.3 us
    pallas_call x1, Pallas kernels, per_device(): pl.pallas_call(write_kernel, out_shape=outs, in_specs=[pl.BlockSpec(memor...  9.22 us

profile of v3, /device:TPU:0, one launch (start us, length us, event | category | flops | bytes accessed | tf_op | source)
XLA Modules:
  0.0 67.1 jit_solution(5924996276792181726)
XLA Ops:
  0.6 57.3 %ewald_block.1 = (bf16[1,128,128]{2,1,0:T(8,128)(2,1)}, bf16[1,128,128]{2,1,0:T(8,128)(2,1)}, f32[128,128]{1,0:T(8,128)}, f32[128,128]{1,0:T(8,128)}, f32[8,128]{1,0:T(8,128)}, /*index=5*/f32[128,128]{1,0:T(8,128)}) custom-call(bf16[1,128,128]{2,1,0:T(8,128)(2,1)} %refs_0_.1, f32[3,1,128]{2,1,0:T(1,128)} %bitcast.2, s32[1,128]{1,0:T(1,128)} %refs_2_.1, ...), custom_call_target="tpu_custom_call" | custom-call | tf_op jit(solution)/shard_map/ewald_block/pallas_call | solution.py:639
  57.9 9.2 %write_out.1 = (bf16[1,128,128]{2,1,0:T(8,128)(2,1)}, bf16[1,128,128]{2,1,0:T(8,128)(2,1)}, f32[128,128]{1,0:T(8,128)}, f32[128,128]{1,0:T(8,128)}, f32[8,128]{1,0:T(8,128)}, /*index=5*/f32[128,128]{1,0:T(8,128)}) custom-call(bf16[1,128,128]{2,1,0:T(8,128)(2,1)} %get-tuple-element.12.refs_0_, bf16[1,128,128]{2,1,0:T(8,128)(2,1)} %get-tuple-element.13.refs_1_, ...), custom_call_target="tpu_custom_call" | custom-call | tf_op jit(solution)/shard_map/write_out/pallas_call | solution.py:650

commit v4 on v3

--- a/solution.py
+++ b/solution.py
@@ -12,10 +12,11 @@
 edge_scale = 0.25
 filter_factor = 12.0
 MESH = pl.DeviceIdType.MESH
-edge_chunk = 1024
+edge_chunk = 2048
 wave_chunk = 128
 lane = 128
-part_rows = 8
+part_rows = 16
+coord_rows = 8
 
 sine_terms = (32.78140079, -74.47800454, 81.36681529, -41.33121431, 6.2830558)
 cosine_terms = (-21.07678176, 58.79403849, -85.27239696, 64.92872661, -19.73898252, 0.99999922)
@@ -92,14 +93,10 @@
     field,
     half_out,
     half_in,
-    sums_a,
-    sums_b,
-    slots_a,
-    slots_b,
-    reduced_a,
-    reduced_b,
-    owned_a,
-    owned_b,
+    sums,
+    slots,
+    reduced,
+    owned,
     gather_send,
     gather_recv,
     pass_send,
@@ -178,8 +175,24 @@
             device_id_type=MESH,
         )
 
-    for copy in loads:
-        copy.wait()
+    for index in (10, 11, 12, 13):
+        loads[index].wait()
+
+    pair_total[...] = jnp.zeros_like(pair_total)
+
+    def edge_step(step, carry):
+        at = pl.ds(pl.multiple_of(step * edge_chunk, edge_chunk), edge_chunk)
+        weights = edge_weights(lengths[:, at], mask[:, at], bases)
+        receiver = spread(receivers[:, at], atoms).astype(jnp.bfloat16)
+        sender = spread(senders[:, at], atoms + 2 * ghosts).astype(jnp.bfloat16)
+        left = jnp.concatenate([receiver * weights[b : b + 1] for b in range(bases)], axis=0)
+        pair_total[...] += by_transpose(left, sender)
+        return carry
+
+    edge_step(0, 0)
+
+    for index in (0, 1, 2, 3, 4, 5, 6, 7, 8, 9, 14, 15, 16):
+        loads[index].wait()
     rows = feats[0]
     upstream_cot = cotangent[0]
     pos_all[me] = jnp.zeros(pos_all.shape[1:], jnp.float32)
@@ -248,30 +261,9 @@
     for copy in ghost_copies:
         copy.start()
 
-    pair_total[...] = jnp.zeros_like(pair_total)
-
-    def edge_step(step, carry):
-        at = pl.ds(pl.multiple_of(step * edge_chunk, edge_chunk), edge_chunk)
-        weights = edge_weights(lengths[:, at], mask[:, at], bases)
-        receiver = spread(receivers[:, at], atoms).astype(jnp.bfloat16)
-        sender = spread(senders[:, at], atoms + 2 * ghosts).astype(jnp.bfloat16)
-        left = jnp.concatenate([receiver * weights[b : b + 1] for b in range(bases)], axis=0)
-        pair_total[...] += by_transpose(left, sender)
-        return carry
-
-    edge_steps = lengths.shape[1] // edge_chunk
-    early_steps = edge_steps * 2 // 3
-    lax.fori_loop(0, early_steps, edge_step, 0)
-    for step in range(1, chips):
-        gather_pass(pos_all, 0, step)
-    for step in range(1, chips):
-        gather_pass(charge_all, 1, step)
-    lax.fori_loop(early_steps, edge_steps, edge_step, 0)
-    pairs[...] = pair_total[...].astype(jnp.bfloat16)
-
     wave_rows[...] = jnp.zeros_like(wave_rows)
     wave_rows[0:3, :] = waves[:, pl.ds(pl.multiple_of(core * half, lane), half)].astype(jnp.float32)
-    ones = jnp.ones((part_rows, lane), jnp.bfloat16)
+    ones = jnp.ones((coord_rows, lane), jnp.bfloat16)
     wave = wave_rows[...]
     squared = rows_by_rows((wave * wave).astype(jnp.bfloat16), ones)
     filt[...] = filter_factor * jnp.exp(-squared * smearing[...]) * lax.rsqrt(squared)
@@ -284,8 +276,7 @@
     def columns(step):
         return pl.ds(pl.multiple_of(step * pair, lane), pair)
 
-    def table_step(step, carry):
-        gather_wait(pos_all, 0, step)
+    def table_block(step):
         block = pos_all[pair_of(step)]
         exact = jnp.concatenate([block[0], block[1]], axis=1)
         first = exact.astype(jnp.bfloat16).astype(jnp.float32)
@@ -302,12 +293,36 @@
             table[half + low_row : half + low_row + wave_chunk, at] = (
                 turns * horner(sine_terms, square)
             ).astype(jnp.bfloat16)
+
+    edge_steps = lengths.shape[1] // edge_chunk
+    alone = 2
+    shared = edge_steps - alone
+    blocks = chips // shared
+    assert blocks * shared == chips
+    edge_step(1, 0)
+    for step in range(1, chips):
+        gather_pass(pos_all, 0, step)
+
+    def shared_step(step, carry):
+        for block in range(blocks):
+            gather_wait(pos_all, 0, step * blocks + block)
+        edge_step(alone + step, carry)
+        for block in range(blocks):
+            table_block(step * blocks + block)
+        return carry
+
+    lax.fori_loop(0, shared // 2, shared_step, 0)
+    for step in range(1, chips):
+        gather_pass(charge_all, 1, step)
+    lax.fori_loop(shared // 2, shared, shared_step, 0)
+    pairs[...] = pair_total[...].astype(jnp.bfloat16)
+
+    def in_steps(buffer, steps):
+        return jnp.concatenate([buffer[chip_at(step) * 2 + c] for step in steps for c in (0, 1)])
+
+    for step in range(chips):
         gather_wait(charge_all, 1, step)
-        structure[...] += plain(table[:, at], charge_all[pair_of(step)].reshape(pair, -1))
-        return carry
-
-    structure[...] = jnp.zeros_like(structure)
-    lax.fori_loop(0, chips, table_step, 0)
+    structure[...] = plain(table[...], in_steps(charge_all, range(chips)))
     own_table[...] = table[:, 0:pair].T
 
     def fill_field(scale):
@@ -364,134 +379,106 @@
     ]
     for copy in return_copies:
         copy.start()
-    sums_a[0:atoms_of(sums_a), :] = rows_by_rows(extended[...], grad_msg)
-    sums_a[atoms_of(sums_a) :, :] = rows_by_rows(act, upstream_cot)
-
-    def scatter_start(sums, slots, which):
-        owners = sums.shape[0] // part_rows
-        slots[linear] = jnp.zeros(slots.shape[1:], jnp.float32)
-
-        def send(step, carry):
-            target = lax.rem(linear + step, devices)
-
-            @pl.when(target < owners)
+    width = rows.shape[1]
+    sums[0:width, :] = rows_by_rows(extended[...], grad_msg).astype(jnp.bfloat16)
+    sums[width : 2 * width, :] = rows_by_rows(act, upstream_cot).astype(jnp.bfloat16)
+    grad_radial = [jnp.sum(mixed[b] * scaled_pre, axis=0, keepdims=True) for b in range(bases)]
+    grad_radial.append(jnp.zeros((part_rows - bases, width), jnp.float32))
+    sums[3 * width :, :] = jnp.concatenate(grad_radial, axis=0).astype(jnp.bfloat16)
+
+    owners = sums.shape[0] // part_rows
+    early = 2 * width // part_rows
+
+    def part(ref, owner):
+        return ref.at[pl.ds(pl.multiple_of(owner * part_rows, part_rows), part_rows)]
+
+    def send_part(owner):
+        return pltpu.make_async_remote_copy(
+            src_ref=part(sums, owner),
+            dst_ref=slots.at[linear],
+            send_sem=weight_send.at[0],
+            recv_sem=weight_recv.at[0],
+            device_id=place(owner),
+            device_id_type=MESH,
+        )
+
+    def scatter_start(first, last):
+        for owner in range(first, last):
+
+            @pl.when(linear != owner)
             def _():
-                pltpu.make_async_remote_copy(
-                    src_ref=sums.at[pl.ds(pl.multiple_of(target * part_rows, part_rows), part_rows)],
-                    dst_ref=slots.at[linear],
-                    send_sem=weight_send.at[which],
-                    recv_sem=weight_recv.at[which],
-                    device_id=place(target),
-                    device_id_type=MESH,
-                ).start()
-
-            return carry
-
-        lax.fori_loop(1, devices, send, 0, unroll=devices <= 32)
-
-    def wait_bytes(ref, send, recv):
+                send_part(owner).start()
+
+    def wait_bytes(ref, which):
         return pltpu.make_async_remote_copy(
             src_ref=ref,
             dst_ref=ref,
-            send_sem=send,
-            recv_sem=recv,
+            send_sem=weight_send.at[which],
+            recv_sem=weight_recv.at[which],
             device_id=(cell, partner),
             device_id_type=MESH,
         )
 
-    def scatter_finish(sums, slots, owned, reduced, which):
-        owners = sums.shape[0] // part_rows
-        mine = pl.ds(pl.multiple_of(lax.rem(linear, owners) * part_rows, part_rows), part_rows)
-        send, recv = weight_send.at[which], weight_recv.at[which]
-
+    def share():
         @pl.when(linear < owners)
         def _():
-            wait_bytes(slots.at[pl.ds(0, devices - 1)], send, recv).wait_recv()
-            wait_bytes(sums.at[pl.ds(0, (owners - 1) * part_rows)], send, recv).wait_send()
-            total = sums[mine, :]
-            for index in range(devices):
-                total += slots[index]
-            owned[...] = total * grad_scale
-            reduced[mine, :] = owned[...]
-
-        @pl.when(linear >= owners)
-        def _():
-            wait_bytes(sums, send, recv).wait_send()
-
-    def share_start(owned, reduced, which):
-        owners = reduced.shape[0] // part_rows
-
-        @pl.when(linear < owners)
-        def _():
+            wait_bytes(slots.at[pl.ds(0, devices - 1)], 0).wait_recv()
+            slots[linear] = part(sums, linear)[...]
+            total = slots[0].astype(jnp.float32)
+            for index in range(1, devices):
+                total += slots[index].astype(jnp.float32)
+            owned[...] = (total * grad_scale).astype(jnp.bfloat16)
+
             def send(step, carry):
-                target = lax.rem(linear + step, devices)
                 pltpu.make_async_remote_copy(
                     src_ref=owned,
-                    dst_ref=reduced.at[
-                        pl.ds(
-                            pl.multiple_of(lax.rem(linear, owners) * part_rows, part_rows),
-                            part_rows,
-                        )
-                    ],
-                    send_sem=weight_send.at[which + 1],
-                    recv_sem=weight_recv.at[which + 1],
-                    device_id=place(target),
+                    dst_ref=part(reduced, linear),
+                    send_sem=weight_send.at[1],
+                    recv_sem=weight_recv.at[1],
+                    device_id=place(lax.rem(linear + step, devices)),
                     device_id_type=MESH,
                 ).start()
                 return carry
 
             lax.fori_loop(1, devices, send, 0, unroll=devices <= 32)
-
-    def share_finish(slots, reduced, which):
-        owners = reduced.shape[0] // part_rows
-        send, recv = weight_send.at[which + 1], weight_recv.at[which + 1]
-
+            part(reduced, linear)[...] = owned[...]
+
+    def share_end():
         @pl.when(linear < owners)
         def _():
-            wait_bytes(reduced.at[pl.ds(0, (owners - 1) * part_rows)], send, recv).wait_recv()
-            wait_bytes(slots.at[pl.ds(0, devices - 1)], send, recv).wait_send()
+            wait_bytes(reduced.at[pl.ds(0, (owners - 1) * part_rows)], 1).wait_recv()
+            wait_bytes(slots.at[pl.ds(0, devices - 1)], 1).wait_send()
+            wait_bytes(sums.at[pl.ds(0, (owners - 1) * part_rows)], 0).wait_send()
 
         @pl.when(linear >= owners)
         def _():
-            wait_bytes(reduced, send, recv).wait_recv()
-
-    scatter_start(sums_a, slots_a, 0)
-
-    grad_radial = jnp.concatenate(
-        [jnp.sum(mixed[b] * scaled_pre, axis=0, keepdims=True) for b in range(bases)], axis=0
-    )
-    sums_b[pl.ds(sums_b.shape[0] - bases, bases), :] = grad_radial
-
-    ahead = min(2, chips - 1)
-    for step in range(1, ahead + 1):
+            wait_bytes(reduced, 1).wait_recv()
+            wait_bytes(sums, 0).wait_send()
+
+    groups = 2
+    size = chips // groups
+    for step in range(1, size):
         gather_pass(grad_all, 2, step)
-    structure[...] = jnp.zeros_like(structure)
-
-    def back_step(step, carry):
-        @pl.when(step + ahead < chips)
-        def _():
-            @pl.when(step > 0)
-            def _():
-                gather_pass(grad_all, 2, step + ahead)
-
-        gather_wait(grad_all, 2, step)
-        structure[...] += plain(
-            table[:, columns(step)], grad_all[pair_of(step)].reshape(pair, -1)
+    for group in range(groups):
+        steps = range(group * size, (group + 1) * size)
+        if group + 1 < groups:
+            for step in range((group + 1) * size, (group + 2) * size):
+                gather_pass(grad_all, 2, step)
+        for step in steps:
+            gather_wait(grad_all, 2, step)
+        update = plain(
+            table[:, group * size * pair : (group + 1) * size * pair], in_steps(grad_all, steps)
         )
-        return carry
-
-    lax.fori_loop(0, chips, back_step, 0)
+        structure[...] = update if group == 0 else structure[...] + update
     fill_field(inv_waves * inv_atoms)
     gather_end(grad_all, 2)
     second_exchange = exchange(1)
 
-    scatter_finish(sums_a, slots_a, owned_a, reduced_a, 0)
-    share_start(owned_a, reduced_a, 0)
-
+    scatter_start(0, early)
     second_exchange.wait()
     grad_raw = ((half_out[1, core] + half_in[1]) * gain).astype(jnp.bfloat16)
-    sums_b[0 : sums_b.shape[0] - bases, :] = rows_by_rows(rows, grad_raw)
-    scatter_start(sums_b, slots_b, 2)
+    sums[2 * width : 3 * width, :] = rows_by_rows(rows, grad_raw).astype(jnp.bfloat16)
+    scatter_start(early, owners)
     for copy in return_copies:
         copy.wait()
     total = (
@@ -503,30 +490,32 @@
     )
     feat_grad_ref[0] = total.astype(jnp.bfloat16)
 
-    scatter_finish(sums_b, slots_b, owned_b, reduced_b, 2)
-    share_start(owned_b, reduced_b, 2)
-    share_finish(slots_a, reduced_a, 0)
-    grad_message_ref[...] = reduced_a[0 : atoms_of(sums_a), :]
-    grad_out_ref[...] = reduced_a[atoms_of(sums_a) :, :]
-    share_finish(slots_b, reduced_b, 2)
-    grad_charge_ref[...] = reduced_b[0 : sums_b.shape[0] - bases, :]
-    grad_radial_ref[...] = reduced_b[sums_b.shape[0] - bases :, :]
-
-
-def atoms_of(sums):
-    return sums.shape[0] // 2
+    share()
+    share_end()
+    final = reduced[...].astype(jnp.float32)
+    grad_message_ref[...] = final[0:width]
+    grad_out_ref[...] = final[width : 2 * width]
+    grad_charge_ref[...] = final[2 * width : 3 * width]
+    grad_radial_ref[...] = final[3 * width : 3 * width + bases]
 
 
 def write_kernel(*refs):
-    done = refs[-1]
-    count = len(refs) // 2
-    copies = [
-        pltpu.make_async_copy(refs[index], refs[count + index], done.at[index])
+    count = len(refs) // 3
+    sources, results, held, done = refs[:count], refs[count : 2 * count], refs[2 * count : -1], refs[-1]
+    first = [
+        pltpu.make_async_copy(sources[index], held[index], done.at[0, index])
         for index in range(count)
     ]
-    for copy in copies:
+    second = [
+        pltpu.make_async_copy(held[index], results[index], done.at[1, index])
+        for index in range(count)
+    ]
+    for copy in first:
         copy.start()
-    for copy in copies:
+    for copy, onward in zip(first, second):
+        copy.wait()
+        onward.start()
+    for copy in second:
         copy.wait()
 
 
@@ -559,10 +548,9 @@
     chips = domains // 2
     f32, bf16 = jnp.float32, jnp.bfloat16
     vmem = pl.BlockSpec(memory_space=pltpu.VMEM)
-    count_a = 2 * width
-    count_b = width + bases
+    count = 3 * width + part_rows
     scratch = [
-        pltpu.VMEM((domains, part_rows, atoms), f32),
+        pltpu.VMEM((domains, coord_rows, atoms), f32),
         pltpu.VMEM((domains, atoms, width), bf16),
         pltpu.VMEM((domains, atoms, width), bf16),
         pltpu.VMEM((2, ghosts, width), bf16),
@@ -573,21 +561,17 @@
         pltpu.VMEM((bases * atoms, atoms + 2 * ghosts), bf16),
         pltpu.VMEM((wave_count // 2, width), f32),
         pltpu.VMEM((wave_count, width), f32),
-        pltpu.VMEM((part_rows, wave_count // 2), f32),
-        pltpu.VMEM((wave_count // 2, 3 * part_rows), bf16),
+        pltpu.VMEM((coord_rows, wave_count // 2), f32),
+        pltpu.VMEM((wave_count // 2, 3 * coord_rows), bf16),
         pltpu.VMEM((wave_count, domains * atoms), bf16),
         pltpu.VMEM((2 * atoms, wave_count), bf16),
         pltpu.VMEM((wave_count, width), bf16),
         pltpu.VMEM((2, 2, atoms, width), f32),
         pltpu.VMEM((2, atoms, width), f32),
-        pltpu.VMEM((count_a, width), f32),
-        pltpu.VMEM((count_b, width), f32),
-        pltpu.VMEM((devices, part_rows, width), f32),
-        pltpu.VMEM((devices, part_rows, width), f32),
-        pltpu.VMEM((count_a, width), f32),
-        pltpu.VMEM((count_b, width), f32),
-        pltpu.VMEM((part_rows, width), f32),
-        pltpu.VMEM((part_rows, width), f32),
+        pltpu.VMEM((count, width), bf16),
+        pltpu.VMEM((devices, part_rows, width), bf16),
+        pltpu.VMEM((count, width), bf16),
+        pltpu.VMEM((part_rows, width), bf16),
         pltpu.SemaphoreType.DMA((3, chips)),
         pltpu.SemaphoreType.DMA((3, chips)),
         pltpu.SemaphoreType.DMA((3, chips)),
@@ -596,8 +580,8 @@
         pltpu.SemaphoreType.DMA((4,)),
         pltpu.SemaphoreType.DMA((2,)),
         pltpu.SemaphoreType.DMA((2,)),
-        pltpu.SemaphoreType.DMA((4,)),
-        pltpu.SemaphoreType.DMA((4,)),
+        pltpu.SemaphoreType.DMA((2,)),
+        pltpu.SemaphoreType.DMA((2,)),
     ]
     shape = jax.ShapeDtypeStruct
     operands = (
@@ -652,7 +636,10 @@
         out_shape=outs,
         in_specs=[pl.BlockSpec(memory_space=pltpu.HBM)] * len(outs),
         out_specs=(pl.BlockSpec(memory_space=pltpu.HBM),) * len(outs),
-        scratch_shapes=[pltpu.SemaphoreType.DMA((len(outs),))],
+        scratch_shapes=[
+            *[pltpu.VMEM(out.shape, out.dtype) for out in outs],
+            pltpu.SemaphoreType.DMA((2, len(outs))),
+        ],
         compiler_params=pltpu.CompilerParams(vmem_limit_bytes=64 * 1024 * 1024),
         name="write_out",
     )(*results)

time: 67.3 us -> 58 us (0.86)
  Pallas kernels: 66.5 us -> 57 us
    pallas_call x1, Pallas kernels: 9.22 us -> 1.68 us  [per_device(): pl.pallas_call(write_kernel, out_shape=outs, in_specs=[pl.BlockSpec(memor...]
    pallas_call x1, Pallas kernels: 57.3 us -> 55.3 us  [per_device(): pl.pallas_call(body, out_shape=outs, in_specs=[pl.BlockSpec(memory_space=...]
where the time goes in v4:
time: 58 us; the launch traced here: 57.8 us
  Pallas kernels  57 us (98%)
  between operations  0.81 us (1%)
    pallas_call x1, Pallas kernels, per_device(): pl.pallas_call(body, out_shape=outs, in_specs=[pl.BlockSpec(memory_space=...  55.3 us
    pallas_call x1, Pallas kernels, per_device(): pl.pallas_call(write_kernel, out_shape=outs, in_specs=[pl.BlockSpec(memor...  1.68 us

profile of v4, /device:TPU:0, one launch (start us, length us, event | category | flops | bytes accessed | tf_op | source)
XLA Modules:
  0.0 57.8 jit_solution(17869640309395163555)
XLA Ops:
  0.6 55.3 %ewald_block.1 = (bf16[1,128,128]{2,1,0:T(8,128)(2,1)}, bf16[1,128,128]{2,1,0:T(8,128)(2,1)}, f32[128,128]{1,0:T(8,128)}, f32[128,128]{1,0:T(8,128)}, f32[8,128]{1,0:T(8,128)}, /*index=5*/f32[128,128]{1,0:T(8,128)}) custom-call(bf16[1,128,128]{2,1,0:T(8,128)(2,1)} %refs_0_.1, f32[3,1,128]{2,1,0:T(1,128)} %bitcast.2, s32[1,128]{1,0:T(1,128)} %refs_2_.1, ...), custom_call_target="tpu_custom_call" | custom-call | tf_op jit(solution)/shard_map/ewald_block/pallas_call | solution.py:623
  55.9 1.7 %write_out.1 = (bf16[1,128,128]{2,1,0:T(8,128)(2,1)}, bf16[1,128,128]{2,1,0:T(8,128)(2,1)}, f32[128,128]{1,0:T(8,128)}, f32[128,128]{1,0:T(8,128)}, f32[8,128]{1,0:T(8,128)}, /*index=5*/f32[128,128]{1,0:T(8,128)}) custom-call(bf16[1,128,128]{2,1,0:T(8,128)(2,1)} %get-tuple-element.12.refs_0_, bf16[1,128,128]{2,1,0:T(8,128)(2,1)} %get-tuple-element.13.refs_1_, ...), custom_call_target="tpu_custom_call" | custom-call | tf_op jit(solution)/shard_map/write_out/pallas_call | solution.py:634

commit v5 on v4

--- a/solution.py
+++ b/solution.py
@@ -12,7 +12,7 @@
 edge_scale = 0.25
 filter_factor = 12.0
 MESH = pl.DeviceIdType.MESH
-edge_chunk = 2048
+edge_chunk = 1024
 wave_chunk = 128
 lane = 128
 part_rows = 16
@@ -175,9 +175,6 @@
             device_id_type=MESH,
         )
 
-    for index in (10, 11, 12, 13):
-        loads[index].wait()
-
     pair_total[...] = jnp.zeros_like(pair_total)
 
     def edge_step(step, carry):
@@ -188,8 +185,6 @@
         left = jnp.concatenate([receiver * weights[b : b + 1] for b in range(bases)], axis=0)
         pair_total[...] += by_transpose(left, sender)
         return carry
-
-    edge_step(0, 0)
 
     for index in (0, 1, 2, 3, 4, 5, 6, 7, 8, 9, 14, 15, 16):
         loads[index].wait()
@@ -260,6 +255,12 @@
     ]
     for copy in ghost_copies:
         copy.start()
+
+    for index in (10, 11, 12, 13):
+        loads[index].wait()
+    edge_steps = lengths.shape[1] // edge_chunk
+    alone = edge_steps // 3
+    lax.fori_loop(0, alone, edge_step, 0)
 
     wave_rows[...] = jnp.zeros_like(wave_rows)
     wave_rows[0:3, :] = waves[:, pl.ds(pl.multiple_of(core * half, lane), half)].astype(jnp.float32)
@@ -294,16 +295,18 @@
                 turns * horner(sine_terms, square)
             ).astype(jnp.bfloat16)
 
-    edge_steps = lengths.shape[1] // edge_chunk
-    alone = 2
     shared = edge_steps - alone
     blocks = chips // shared
     assert blocks * shared == chips
-    edge_step(1, 0)
     for step in range(1, chips):
         gather_pass(pos_all, 0, step)
 
     def shared_step(step, carry):
+        @pl.when(step == shared // 4)
+        def _():
+            for back in range(1, chips):
+                gather_pass(charge_all, 1, back)
+
         for block in range(blocks):
             gather_wait(pos_all, 0, step * blocks + block)
         edge_step(alone + step, carry)
@@ -311,18 +314,36 @@
             table_block(step * blocks + block)
         return carry
 
-    lax.fori_loop(0, shared // 2, shared_step, 0)
-    for step in range(1, chips):
-        gather_pass(charge_all, 1, step)
-    lax.fori_loop(shared // 2, shared, shared_step, 0)
+    lax.fori_loop(0, shared, shared_step, 0)
     pairs[...] = pair_total[...].astype(jnp.bfloat16)
 
-    def in_steps(buffer, steps):
-        return jnp.concatenate([buffer[chip_at(step) * 2 + c] for step in steps for c in (0, 1)])
-
-    for step in range(chips):
-        gather_wait(charge_all, 1, step)
-    structure[...] = plain(table[...], in_steps(charge_all, range(chips)))
+    size = 2
+
+    def structure_sums(buffer, which, passing):
+        structure[...] = jnp.zeros_like(structure)
+
+        def group_step(group, carry):
+            if passing:
+                for j in range(size):
+                    later = (group + 1) * size + j
+
+                    @pl.when(later < chips)
+                    def _():
+                        gather_pass(buffer, which, later)
+
+            for j in range(size):
+                gather_wait(buffer, which, group * size + j)
+            block = jnp.concatenate(
+                [buffer[chip_at(group * size + j) * 2 + c] for j in range(size) for c in (0, 1)]
+            )
+            wide = size * pair
+            at = pl.ds(pl.multiple_of(group * wide, lane), wide)
+            structure[...] += plain(table[:, at], block)
+            return carry
+
+        lax.fori_loop(0, chips // size, group_step, 0)
+
+    structure_sums(charge_all, 1, False)
     own_table[...] = table[:, 0:pair].T
 
     def fill_field(scale):
@@ -455,21 +476,9 @@
             wait_bytes(reduced, 1).wait_recv()
             wait_bytes(sums, 0).wait_send()
 
-    groups = 2
-    size = chips // groups
     for step in range(1, size):
         gather_pass(grad_all, 2, step)
-    for group in range(groups):
-        steps = range(group * size, (group + 1) * size)
-        if group + 1 < groups:
-            for step in range((group + 1) * size, (group + 2) * size):
-                gather_pass(grad_all, 2, step)
-        for step in steps:
-            gather_wait(grad_all, 2, step)
-        update = plain(
-            table[:, group * size * pair : (group + 1) * size * pair], in_steps(grad_all, steps)
-        )
-        structure[...] = update if group == 0 else structure[...] + update
+    structure_sums(grad_all, 2, True)
     fill_field(inv_waves * inv_atoms)
     gather_end(grad_all, 2)
     second_exchange = exchange(1)

time: 58 us -> 55.2 us (0.952)
  Pallas kernels: 57 us -> 54.3 us
    pallas_call x1, Pallas kernels: 55.3 us -> 52.6 us  [per_device(): pl.pallas_call(body, out_shape=outs, in_specs=[pl.BlockSpec(memory_space=...]
where the time goes in v5:
time: 55.2 us; the launch traced here: 55 us
  Pallas kernels  54.3 us (98%)
  between operations  0.65 us (1%)
    pallas_call x1, Pallas kernels, per_device(): pl.pallas_call(body, out_shape=outs, in_specs=[pl.BlockSpec(memory_space=...  52.6 us
    pallas_call x1, Pallas kernels, per_device(): pl.pallas_call(write_kernel, out_shape=outs, in_specs=[pl.BlockSpec(memor...  1.68 us

profile of v5, /device:TPU:0, one launch (start us, length us, event | category | flops | bytes accessed | tf_op | source)
XLA Modules:
  0.0 55.0 jit_solution(15104080346926754106)
XLA Ops:
  0.6 52.6 %ewald_block.1 = (bf16[1,128,128]{2,1,0:T(8,128)(2,1)}, bf16[1,128,128]{2,1,0:T(8,128)(2,1)}, f32[128,128]{1,0:T(8,128)}, f32[128,128]{1,0:T(8,128)}, f32[8,128]{1,0:T(8,128)}, /*index=5*/f32[128,128]{1,0:T(8,128)}) custom-call(bf16[1,128,128]{2,1,0:T(8,128)(2,1)} %refs_0_.1, f32[3,1,128]{2,1,0:T(1,128)} %bitcast.2, s32[1,128]{1,0:T(1,128)} %refs_2_.1, ...), custom_call_target="tpu_custom_call" | custom-call | tf_op jit(solution)/shard_map/ewald_block/pallas_call | solution.py:632
  53.3 1.7 %write_out.1 = (bf16[1,128,128]{2,1,0:T(8,128)(2,1)}, bf16[1,128,128]{2,1,0:T(8,128)(2,1)}, f32[128,128]{1,0:T(8,128)}, f32[128,128]{1,0:T(8,128)}, f32[8,128]{1,0:T(8,128)}, /*index=5*/f32[128,128]{1,0:T(8,128)}) custom-call(bf16[1,128,128]{2,1,0:T(8,128)(2,1)} %get-tuple-element.12.refs_0_, bf16[1,128,128]{2,1,0:T(8,128)(2,1)} %get-tuple-element.13.refs_1_, ...), custom_call_target="tpu_custom_call" | custom-call | tf_op jit(solution)/shard_map/write_out/pallas_call | solution.py:643

commit v6 on v5

--- a/solution.py
+++ b/solution.py
@@ -18,8 +18,8 @@
 part_rows = 16
 coord_rows = 8
 
-sine_terms = (32.78140079, -74.47800454, 81.36681529, -41.33121431, 6.2830558)
-cosine_terms = (-21.07678176, 58.79403849, -85.27239696, 64.92872661, -19.73898252, 0.99999922)
+sine_terms = (-0.784374028, 3.59478808, -7.30744342, 4.4428679)
+cosine_terms = (-1.72834866, 5.7152384, -6.97764206, 1.41420408)
 
 
 def horner(terms, x):
@@ -175,7 +175,6 @@
             device_id_type=MESH,
         )
 
-    pair_total[...] = jnp.zeros_like(pair_total)
 
     def edge_step(step, carry):
         at = pl.ds(pl.multiple_of(step * edge_chunk, edge_chunk), edge_chunk)
@@ -201,6 +200,15 @@
     outgoing[1] = rows_by_rows(down_spread, rows).astype(jnp.bfloat16)
     extended[0:atoms, :] = rows
 
+    wave_rows[...] = jnp.zeros_like(wave_rows)
+    wave_rows[0:3, :] = waves[:, pl.ds(pl.multiple_of(core * half, lane), half)].astype(jnp.float32)
+    ones = jnp.ones((coord_rows, lane), jnp.bfloat16)
+    wave = wave_rows[...]
+    squared = rows_by_rows((wave * wave).astype(jnp.bfloat16), ones)
+    filt[...] = filter_factor * jnp.exp(-squared * smearing[...]) * lax.rsqrt(squared)
+    wave_columns[...] = jnp.concatenate([wave, wave, wave], axis=0).T.astype(jnp.bfloat16)
+    pair_total[...] = jnp.zeros_like(pair_total)
+
     pl.semaphore_wait(barrier, devices - 1)
 
     def gather_copy(buffer, which, step, index):
@@ -262,13 +270,6 @@
     alone = edge_steps // 3
     lax.fori_loop(0, alone, edge_step, 0)
 
-    wave_rows[...] = jnp.zeros_like(wave_rows)
-    wave_rows[0:3, :] = waves[:, pl.ds(pl.multiple_of(core * half, lane), half)].astype(jnp.float32)
-    ones = jnp.ones((coord_rows, lane), jnp.bfloat16)
-    wave = wave_rows[...]
-    squared = rows_by_rows((wave * wave).astype(jnp.bfloat16), ones)
-    filt[...] = filter_factor * jnp.exp(-squared * smearing[...]) * lax.rsqrt(squared)
-    wave_columns[...] = jnp.concatenate([wave, wave, wave], axis=0).T.astype(jnp.bfloat16)
     pair = 2 * atoms
 
     def pair_of(step):
@@ -290,9 +291,10 @@
             turns = plain(wave_columns[piece, :], points)
             turns = turns - jnp.floor(turns + 0.5)
             square = turns * turns
-            table[piece, at] = horner(cosine_terms, square).astype(jnp.bfloat16)
+            sine = turns * horner(sine_terms, square)
+            table[piece, at] = (1.0 - sine * sine).astype(jnp.bfloat16)
             table[half + low_row : half + low_row + wave_chunk, at] = (
-                turns * horner(sine_terms, square)
+                sine * horner(cosine_terms, square)
             ).astype(jnp.bfloat16)
 
     shared = edge_steps - alone

time: 55.2 us -> 54.3 us (0.984)
  Pallas kernels: 54.3 us -> 53.4 us
    pallas_call x1, Pallas kernels: 52.6 us -> 51.8 us  [per_device(): pl.pallas_call(body, out_shape=outs, in_specs=[pl.BlockSpec(memory_space=...]
where the time goes in v6:
time: 54.3 us; the launch traced here: 54.1 us
  Pallas kernels  53.4 us (98%)
  between operations  0.65 us (1%)
    pallas_call x1, Pallas kernels, per_device(): pl.pallas_call(body, out_shape=outs, in_specs=[pl.BlockSpec(memory_space=...  51.8 us
    pallas_call x1, Pallas kernels, per_device(): pl.pallas_call(write_kernel, out_shape=outs, in_specs=[pl.BlockSpec(memor...  1.68 us

profile of v6, /device:TPU:0, one launch (start us, length us, event | category | flops | bytes accessed | tf_op | source)
XLA Modules:
  0.0 54.1 jit_solution(5584858050220107115)
XLA Ops:
  0.6 51.8 %ewald_block.1 = (bf16[1,128,128]{2,1,0:T(8,128)(2,1)}, bf16[1,128,128]{2,1,0:T(8,128)(2,1)}, f32[128,128]{1,0:T(8,128)}, f32[128,128]{1,0:T(8,128)}, f32[8,128]{1,0:T(8,128)}, /*index=5*/f32[128,128]{1,0:T(8,128)}) custom-call(bf16[1,128,128]{2,1,0:T(8,128)(2,1)} %refs_0_.1, f32[3,1,128]{2,1,0:T(1,128)} %bitcast.2, s32[1,128]{1,0:T(1,128)} %refs_2_.1, ...), custom_call_target="tpu_custom_call" | custom-call | tf_op jit(solution)/shard_map/ewald_block/pallas_call | solution.py:634
  52.4 1.7 %write_out.1 = (bf16[1,128,128]{2,1,0:T(8,128)(2,1)}, bf16[1,128,128]{2,1,0:T(8,128)(2,1)}, f32[128,128]{1,0:T(8,128)}, f32[128,128]{1,0:T(8,128)}, f32[8,128]{1,0:T(8,128)}, /*index=5*/f32[128,128]{1,0:T(8,128)}) custom-call(bf16[1,128,128]{2,1,0:T(8,128)(2,1)} %get-tuple-element.12.refs_0_, bf16[1,128,128]{2,1,0:T(8,128)(2,1)} %get-tuple-element.13.refs_1_, ...), custom_call_target="tpu_custom_call" | custom-call | tf_op jit(solution)/shard_map/write_out/pallas_call | solution.py:645
